TPU v7x, 512 devices: a whole 4x4x16 slice. The times are simulated.
512 devices in a mesh: row: 16 (over y, x_hi, core), col: 32 (over z, x_lo).
Axes of the slice: x: 4 (x_hi: 2, x_lo: 2; x = x_hi * 2 + x_lo), y: 4, z: 16, core: 2. Of those that a mesh axis runs over, the one named last changes fastest.
Arguments:
- queries: bfloat16 [65536, 32, 128], P(('col', 'row')), may hold values from -100 to 100
- rotated_key_rows: bfloat16 [65536, 4, 128], P(('col', 'row')), may hold values from -6 to 6
- value_matrix_rows: bfloat16 [65536, 4, 128], P(('col', 'row')), may hold values from -6 to 6
- doc_start: int32 [65536], P(('col', 'row')), may hold values from 0 to 65535, as said below
- block_keep: int32 [512, 512], P(('col', 'row')), may hold values 0 or 1
Outputs:
- attention_out: bfloat16 [65536, 32, 128], P(('col', 'row'))
Inputs may be any that keep to these rules, and one draw needn't show every extreme that they name: doc_start[p] is the first position of the document that holds token p; documents are runs of consecutive positions of 1 to 2048 tokens, and at least one holds exactly 2048.
All inputs are finite; a program needn't handle non-finite values. No bound on the sum of `block_keep` on one device may be relied on, other than what follows from the above.
Results may differ from a plain program's by a relative error of at most 0.005.
Values may be sent and summed in bfloat16 or wider, within the bound.
A program may use at most 64 MiB of HBM per device.

v0:
```python
import math

import jax
import jax.numpy as jnp
from jax import lax
from jax.sharding import PartitionSpec as P

NEGATIVE_FILL = -1e30


def from_behind(array, axis, by):
    size = lax.axis_size(axis)
    pairs = [(i, i + by) for i in range(size) if 0 <= i + by < size]
    return lax.ppermute(array, axis, pairs)


def update(carried, key_part, value_part, start_part, key_pos, context):
    grouped, query_starts, query_pos, keep_row, own_block, block_rows, doc_reach, by_documents = (
        context
    )
    key_span = key_part.shape[0]
    per_shard = min(key_span, block_rows)
    picked = lax.dynamic_slice(keep_row, (key_pos[0] // block_rows,), (key_span // per_shard,))
    keep_tok = jnp.repeat(picked, per_shard)
    same_block = key_pos // block_rows == own_block
    allowed = (keep_tok == 1) | same_block
    visible = (query_starts[:, None] == start_part[None, :]) & (
        key_pos[None, :] <= query_pos[:, None]
    )
    visible = visible & allowed[None, :]
    score_scale = 1.0 / math.sqrt(key_part.shape[-1])

    def compute(current):
        running_max, weight_total, attended = current
        scores = (
            jnp.einsum("qhgd,khd->hgqk", grouped, key_part, preferred_element_type=jnp.float32)
            * score_scale
        )
        masked = jnp.where(visible, scores, NEGATIVE_FILL)
        new_max = jnp.maximum(running_max, jnp.max(masked, axis=-1))
        weights = jnp.where(visible, jnp.exp(scores - new_max[..., None]), 0.0)
        factor = jnp.exp(running_max - new_max)
        weight_total = weight_total * factor + jnp.sum(weights, axis=-1)
        product = jnp.einsum(
            "hgqk,khd->hgqd",
            weights.astype(jnp.bfloat16),
            value_part,
            preferred_element_type=jnp.float32,
        )
        attended = attended * factor[..., None] + product
        return (new_max, weight_total, attended)

    needed = (key_pos[0] <= query_pos[-1]) & (key_pos[-1] > query_pos[0] - doc_reach)
    return lax.cond(needed, compute, lambda unchanged: unchanged, carried)


def fold_piece(carried, piece, base_pos, context):
    key_rows, value_rows, start_rows = piece
    row_total = key_rows.shape[0]
    key_span = math.gcd(row_total, 256)
    steps_count = row_total // key_span

    def advance(number, current):
        offset = number * key_span
        key_part = lax.dynamic_slice_in_dim(key_rows, offset, key_span, 0)
        value_part = lax.dynamic_slice_in_dim(value_rows, offset, key_span, 0)
        start_part = lax.dynamic_slice_in_dim(start_rows, offset, key_span, 0)
        key_pos = base_pos + offset + jnp.arange(key_span, dtype=jnp.int32)
        return update(current, key_part, value_part, start_part, key_pos, context)

    return lax.fori_loop(0, steps_count, advance, carried)


def local(queries, rotated_key_rows, value_matrix_rows, doc_start, block_keep):
    row_count = lax.axis_size("row")
    block_rows = queries.shape[0]
    query_heads = queries.shape[1]
    kv_heads = rotated_key_rows.shape[1]
    head_width = queries.shape[2]
    group_size = query_heads // kv_heads
    own_row = lax.axis_index("row")
    own_col = lax.axis_index("col")
    own_block = own_col * row_count + own_row
    doc_reach = row_count * block_rows
    query_pos = own_block * block_rows + jnp.arange(block_rows, dtype=jnp.int32)
    grouped = queries.reshape(block_rows, kv_heads, group_size, head_width)
    starts_next = doc_start + 1
    context = (
        grouped,
        starts_next,
        query_pos,
        block_keep[0],
        own_block,
        block_rows,
        doc_reach,
        False,
    )
    carried = (
        jnp.full((kv_heads, group_size, block_rows), NEGATIVE_FILL, jnp.float32),
        jnp.zeros((kv_heads, group_size, block_rows), jnp.float32),
        jnp.zeros((kv_heads, group_size, block_rows, head_width), jnp.float32),
    )
    own_base = own_col * doc_reach
    prior_base = own_base - doc_reach
    earlier = from_behind((rotated_key_rows, value_matrix_rows, starts_next), "col", 1)
    carried = fold_piece(
        carried,
        (
            lax.all_gather(rotated_key_rows, "row", axis=0, tiled=True),
            lax.all_gather(value_matrix_rows, "row", axis=0, tiled=True),
            lax.all_gather(starts_next, "row", axis=0, tiled=True),
        ),
        own_base,
        context,
    )
    carried = fold_piece(
        carried,
        (
            lax.all_gather(earlier[0], "row", axis=0, tiled=True),
            lax.all_gather(earlier[1], "row", axis=0, tiled=True),
            lax.all_gather(earlier[2], "row", axis=0, tiled=True),
        ),
        prior_base,
        context,
    )
    running_max, weight_total, attended = carried
    result = attended / weight_total[..., None]
    return (
        result.transpose(2, 0, 1, 3)
        .reshape(block_rows, query_heads, head_width)
        .astype(jnp.bfloat16)
    )


def solution(mesh):
    return jax.shard_map(
        local,
        mesh=mesh,
        in_specs=(
            P(("col", "row"), None, None),
            P(("col", "row"), None, None),
            P(("col", "row"), None, None),
            P(("col", "row")),
            P(("col", "row"), None),
        ),
        out_specs=P(("col", "row"), None, None),
        check_vma=False,
    )
```

profile of v0, /device:TPU:1, one launch (start us, length us, event | category | flops | bytes accessed | tf_op | source)
XLA Modules:
  0.0 375.7 jit_solution(9237105162655232860)
XLA Ops:
  6.5 1.6 copy.16
  8.2 1.6 copy.18
  9.8 4.0 %collective-permute-start.1 = (bf16[128,4,128]{2,0,1:T(8,128)(2,1)}, bf16[128,4,128]{2,0,1:T(8,128)(2,1)S(1)}, u32[]{:S(2)}, u32[]{:S(2)}) collective-permute-start(bf16[128,4,128]{2,0,1:T(8,128)(2,1)} %copy.16), channel_id=1, source_target_pairs={{0,1},{1,2},{2,3},{3,4},{4,5},{5,6},{6,7},{7,8},{8,9},{9,10},{10,1... | collective-permute-start | bytes 393224 | tf_op jit(solution)/shard_map/ppermute | solution.py:14
  13.8 2.2 collective-permute-done.1
  16.8 3.7 collective-permute-start.2
  20.5 2.2 collective-permute-done.2
  24.1 4.9 %collective-permute-start = (s32[128]{0:T(128)S(1)}, s32[128]{0:T(128)S(1)}, u32[]{:S(2)}, u32[]{:S(2)}) collective-permute-start(s32[128]{0:T(128)S(1)} %get-tuple-element.2025), channel_id=1, source_target_pairs={{0,1},{1,2},{2,3},{3,4},{4,5},{5,6},{6,7},{7,8},{8,9},{9,10},{10,1... | collective-permute-start | bytes 1544 | tf_op jit(solution)/shard_map/ppermute | solution.py:14
  29.0 26.8 %all-gather = s32[16,1,128]{2,1,0:T(1,128)S(1)} all-gather(s32[1,1,128]{2,1,0:T(1,128)S(1)} %get-tuple-element.1763), channel_id=1, replica_groups=mesh['row'=16,'col'=32] {'row'}, dimensions={0}, use_global_device_ids=true | all-gather | bytes 8704 | tf_op jit(solution)/shard_map/all_gather | solution.py:111
  55.8 1.6 copy.17
  57.5 19.4 %all-gather.1 = s32[16,1,128]{2,1,0:T(1,128)S(1)} all-gather(s32[1,1,128]{2,1,0:T(1,128)S(1)} %bitcast.112), channel_id=1, replica_groups=mesh['row'=16,'col'=32] {'row'}, dimensions={0}, use_global_device_ids=true | all-gather | bytes 8704 | tf_op jit(solution)/shard_map/all_gather | solution.py:121
  76.9 2.4 all-gather.7.cloned.1.call-done
  79.3 65.1 %all-gather.9.cloned.1.call-done = bf16[2048,4,128]{2,0,1:T(8,128)(2,1)} async-done(((bf16[128,4,128]{2,0,1:T(8,128)(2,1)}), bf16[2048,4,128]{2,0,1:T(8,128)(2,1)}) %all-gather.9.cloned.1.call-update) | async-done | bytes 2097168 | tf_op jit(solution)/shard_map/all_gather | solution.py:110
  144.7 32.6 %while.40 = (s32[]{:T(128)}, f32[4,8,128]{2,1,0:T(8,128)S(1)}, f32[4,8,128]{2,1,0:T(8,128)S(1)}, f32[4,8,128,128]{3,2,1,0:T(8,128)S(1)}, s32[]{:T(128)}, /*index...) while((s32[]{:T(128)}, f32[4,8,128]{2,1,0:T(8,128)S(1)}, ...), condition=%wide.region_5.6_spmd, body=%wide.region_0.5_spmd.sunk | while | flops 549597952 | bytes 18754236 | solution.py:71
  147.8 8.3 %conditional.4 = ((f32[4,8,128]{2,1,0:T(8,128)S(1)}, f32[4,8,128]{2,1,0:T(8,128)S(1)}, f32[4,8,128,128]{3,2,1,0:T(8,128)S(1)})) conditional(s32[]{:T(128)} %convert_element_type.63, (f32[4,8,128]{2,1,0:T(8,128)S(1)}, f32[4,8,128]{2,1,0:T(8,128)S(1)}, f32[4,8,128,128]{3,2,1,0:T(8,128)S(1)}) %tuple.162, (s32[128]{0:T(128)S(1)}, s32[]{:T(128)}, ...), branch_computations={%region_1.1_spmd, %region_2.4_spmd.clone} | conditional | flops 549597696 | bytes 18751778 | solution.py:54
  150.8 1.7 fusion
  152.5 0.9 fusion.4
  153.4 2.7 multiply_add_fusion
  177.4 32.3 %all-gather.11.cloned.1.call-done = bf16[2048,4,128]{2,0,1:T(8,128)(2,1)} async-done(((bf16[128,4,128]{2,0,1:T(8,128)(2,1)}), bf16[2048,4,128]{2,0,1:T(8,128)(2,1)}) %all-gather.11.cloned.1.call-update) | async-done | bytes 2097168 | tf_op jit(solution)/shard_map/all_gather | solution.py:119
  209.7 64.9 %all-gather.13.cloned.1.call-done = bf16[2048,4,128]{2,0,1:T(8,128)(2,1)} async-done(((bf16[128,4,128]{2,0,1:T(8,128)(2,1)}), bf16[2048,4,128]{2,0,1:T(8,128)(2,1)}) %all-gather.13.cloned.1.call-update) | async-done | bytes 2097168 | tf_op jit(solution)/shard_map/all_gather | solution.py:120
  274.6 92.1 %while.41 = (s32[]{:T(128)}, f32[4,8,128]{2,1,0:T(8,128)S(1)}, f32[4,8,128]{2,1,0:T(8,128)S(1)}, f32[4,8,128,128]{3,2,1,0:T(8,128)S(1)}, s32[]{:T(128)}, /*index...) while((s32[]{:T(128)}, f32[4,8,128]{2,1,0:T(8,128)S(1)}, ...), condition=%wide.region_11.12_spmd, body=%wide.region_6.11_spmd.sunk | while | flops 549597952 | bytes 18754236 | solution.py:71
  277.8 8.3 %conditional.5 = ((f32[4,8,128]{2,1,0:T(8,128)S(1)}, f32[4,8,128]{2,1,0:T(8,128)S(1)}, f32[4,8,128,128]{3,2,1,0:T(8,128)S(1)})) conditional(s32[]{:T(128)} %convert_element_type.64, (f32[4,8,128]{2,1,0:T(8,128)S(1)}, f32[4,8,128]{2,1,0:T(8,128)S(1)}, f32[4,8,128,128]{3,2,1,0:T(8,128)S(1)}) %tuple.166, (s32[128]{0:T(128)S(1)}, s32[]{:T(128)}, ...), branch_computations={%region_7.7_spmd, %region_8.10_spmd.clone} | conditional | flops 549597696 | bytes 18751778 | solution.py:54
  280.8 1.7 fusion.23
  282.5 0.9 fusion.27
  283.4 2.7 multiply_add_fusion.2
  289.3 8.3 %conditional.5 = ((f32[4,8,128]{2,1,0:T(8,128)S(1)}, f32[4,8,128]{2,1,0:T(8,128)S(1)}, f32[4,8,128,128]{3,2,1,0:T(8,128)S(1)})) conditional(s32[]{:T(128)} %convert_element_type.64, (f32[4,8,128]{2,1,0:T(8,128)S(1)}, f32[4,8,128]{2,1,0:T(8,128)S(1)}, f32[4,8,128,128]{3,2,1,0:T(8,128)S(1)}) %tuple.166, (s32[128]{0:T(128)S(1)}, s32[]{:T(128)}, ...), branch_computations={%region_7.7_spmd, %region_8.10_spmd.clone} | conditional | flops 549597696 | bytes 18751778 | solution.py:54
  292.3 1.7 fusion.23
  294.0 0.9 fusion.27
  294.9 2.7 multiply_add_fusion.2
  300.8 8.3 %conditional.5 = ((f32[4,8,128]{2,1,0:T(8,128)S(1)}, f32[4,8,128]{2,1,0:T(8,128)S(1)}, f32[4,8,128,128]{3,2,1,0:T(8,128)S(1)})) conditional(s32[]{:T(128)} %convert_element_type.64, (f32[4,8,128]{2,1,0:T(8,128)S(1)}, f32[4,8,128]{2,1,0:T(8,128)S(1)}, f32[4,8,128,128]{3,2,1,0:T(8,128)S(1)}) %tuple.166, (s32[128]{0:T(128)S(1)}, s32[]{:T(128)}, ...), branch_computations={%region_7.7_spmd, %region_8.10_spmd.clone} | conditional | flops 549597696 | bytes 18751778 | solution.py:54
  303.8 1.7 fusion.23
  305.5 0.9 fusion.27
  306.5 2.7 multiply_add_fusion.2
  312.4 8.3 %conditional.5 = ((f32[4,8,128]{2,1,0:T(8,128)S(1)}, f32[4,8,128]{2,1,0:T(8,128)S(1)}, f32[4,8,128,128]{3,2,1,0:T(8,128)S(1)})) conditional(s32[]{:T(128)} %convert_element_type.64, (f32[4,8,128]{2,1,0:T(8,128)S(1)}, f32[4,8,128]{2,1,0:T(8,128)S(1)}, f32[4,8,128,128]{3,2,1,0:T(8,128)S(1)}) %tuple.166, (s32[128]{0:T(128)S(1)}, s32[]{:T(128)}, ...), branch_computations={%region_7.7_spmd, %region_8.10_spmd.clone} | conditional | flops 549597696 | bytes 18751778 | solution.py:54
  315.3 1.7 fusion.23
  318.0 2.7 multiply_add_fusion.2
  323.9 8.3 %conditional.5 = ((f32[4,8,128]{2,1,0:T(8,128)S(1)}, f32[4,8,128]{2,1,0:T(8,128)S(1)}, f32[4,8,128,128]{3,2,1,0:T(8,128)S(1)})) conditional(s32[]{:T(128)} %convert_element_type.64, (f32[4,8,128]{2,1,0:T(8,128)S(1)}, f32[4,8,128]{2,1,0:T(8,128)S(1)}, f32[4,8,128,128]{3,2,1,0:T(8,128)S(1)}) %tuple.166, (s32[128]{0:T(128)S(1)}, s32[]{:T(128)}, ...), branch_computations={%region_7.7_spmd, %region_8.10_spmd.clone} | conditional | flops 549597696 | bytes 18751778 | solution.py:54
  326.9 1.7 fusion.23
  329.5 2.7 multiply_add_fusion.2
  335.4 8.3 %conditional.5 = ((f32[4,8,128]{2,1,0:T(8,128)S(1)}, f32[4,8,128]{2,1,0:T(8,128)S(1)}, f32[4,8,128,128]{3,2,1,0:T(8,128)S(1)})) conditional(s32[]{:T(128)} %convert_element_type.64, (f32[4,8,128]{2,1,0:T(8,128)S(1)}, f32[4,8,128]{2,1,0:T(8,128)S(1)}, f32[4,8,128,128]{3,2,1,0:T(8,128)S(1)}) %tuple.166, (s32[128]{0:T(128)S(1)}, s32[]{:T(128)}, ...), branch_computations={%region_7.7_spmd, %region_8.10_spmd.clone} | conditional | flops 549597696 | bytes 18751778 | solution.py:54
  338.4 1.7 fusion.23
  341.0 2.7 multiply_add_fusion.2
  346.9 8.3 %conditional.5 = ((f32[4,8,128]{2,1,0:T(8,128)S(1)}, f32[4,8,128]{2,1,0:T(8,128)S(1)}, f32[4,8,128,128]{3,2,1,0:T(8,128)S(1)})) conditional(s32[]{:T(128)} %convert_element_type.64, (f32[4,8,128]{2,1,0:T(8,128)S(1)}, f32[4,8,128]{2,1,0:T(8,128)S(1)}, f32[4,8,128,128]{3,2,1,0:T(8,128)S(1)}) %tuple.166, (s32[128]{0:T(128)S(1)}, s32[]{:T(128)}, ...), branch_computations={%region_7.7_spmd, %region_8.10_spmd.clone} | conditional | flops 549597696 | bytes 18751778 | solution.py:54
  349.9 1.7 fusion.23
  352.5 2.7 multiply_add_fusion.2
  358.4 8.3 %conditional.5 = ((f32[4,8,128]{2,1,0:T(8,128)S(1)}, f32[4,8,128]{2,1,0:T(8,128)S(1)}, f32[4,8,128,128]{3,2,1,0:T(8,128)S(1)})) conditional(s32[]{:T(128)} %convert_element_type.64, (f32[4,8,128]{2,1,0:T(8,128)S(1)}, f32[4,8,128]{2,1,0:T(8,128)S(1)}, f32[4,8,128,128]{3,2,1,0:T(8,128)S(1)}) %tuple.166, (s32[128]{0:T(128)S(1)}, s32[]{:T(128)}, ...), branch_computations={%region_7.7_spmd, %region_8.10_spmd.clone} | conditional | flops 549597696 | bytes 18751778 | solution.py:54
  361.4 1.7 fusion.23
  364.1 2.7 multiply_add_fusion.2
  367.5 1.6 copy.33
  (169 shorter events, 31.3 us)
Async XLA Ops:
  6.5 138.2 %copy-start.2 = (s32[1,512]{1,0:T(1,128)S(1)}, s32[1,512]{1,0:T(1,128)}, u32[]{:S(2)}) copy-start(s32[1,512]{1,0:T(1,128)} %param.17) | copy-start | bytes 6148
  6.5 72.8 %all-gather.7.cloned.1.call-start = ((), (), s32[]{:S(2)}) async-start(), calls=%async_computation | async-start | bytes 2228224 | tf_op jit(solution)/shard_map/all_gather | solution.py:109
  8.2 136.3 %all-gather.9.cloned.1.call-start = ((), (), s32[]{:S(2)}) async-start(), calls=%async_computation.1 | async-start | bytes 2228224 | tf_op jit(solution)/shard_map/all_gather | solution.py:110
  9.8 199.9 %all-gather.11.cloned.1.call-start = ((), (), s32[]{:S(2)}) async-start(), calls=%async_computation.2 | async-start | bytes 2228224 | tf_op jit(solution)/shard_map/all_gather | solution.py:119
  9.8 6.2 %collective-permute-start.1 = (bf16[128,4,128]{2,0,1:T(8,128)(2,1)}, bf16[128,4,128]{2,0,1:T(8,128)(2,1)S(1)}, u32[]{:S(2)}, u32[]{:S(2)}) collective-permute-start(bf16[128,4,128]{2,0,1:T(8,128)(2,1)} %copy.16), channel_id=1, source_target_pairs={{0,1},{1,2},{2,3},{3,4},{4,5},{5,6},{6,7},{7,8},{8,9},{9,10},{10,1... | collective-permute-start | bytes 393224 | tf_op jit(solution)/shard_map/ppermute | solution.py:14
  16.0 0.7 copy-start
  16.7 257.9 %all-gather.13.cloned.1.call-start = ((), (), s32[]{:S(2)}) async-start(), calls=%async_computation.3 | async-start | bytes 2228224 | tf_op jit(solution)/shard_map/all_gather | solution.py:120
  16.8 6.0 %collective-permute-start.2 = (bf16[128,4,128]{2,0,1:T(8,128)(2,1)}, bf16[128,4,128]{2,0,1:T(8,128)(2,1)S(1)}, u32[]{:S(2)}, u32[]{:S(2)}) collective-permute-start(bf16[128,4,128]{2,0,1:T(8,128)(2,1)} %copy.18), channel_id=1, source_target_pairs={{0,1},{1,2},{2,3},{3,4},{4,5},{5,6},{6,7},{7,8},{8,9},{9,10},{10,1... | collective-permute-start | bytes 393224 | tf_op jit(solution)/shard_map/ppermute | solution.py:14
  22.8 0.6 copy-start.1
  24.1 33.4 %collective-permute-start = (s32[128]{0:T(128)S(1)}, s32[128]{0:T(128)S(1)}, u32[]{:S(2)}, u32[]{:S(2)}) collective-permute-start(s32[128]{0:T(128)S(1)} %get-tuple-element.2025), channel_id=1, source_target_pairs={{0,1},{1,2},{2,3},{3,4},{4,5},{5,6},{6,7},{7,8},{8,9},{9,10},{10,1... | collective-permute-start | bytes 1544 | tf_op jit(solution)/shard_map/ppermute | solution.py:14
Sparse Core Ops, SparseCore 0:
  10.7 68.5 all-gather.6
  82.7 61.7 all-gather.8
  147.8 61.8 all-gather.10
  212.9 61.7 all-gather.12
where the time goes:
time: 377 us; the launch traced here: 376 us
  waiting for transfers between devices  169 us (45%)
  loops' own time  53.8 us (14%)
  blocking collectives  46.2 us (12%)
  matrix products  39.3 us (10%)
  local copies, waits for them, and re-layouts  28.8 us (8%)
  between operations  13.3 us (4%)
  starting transfers between devices  12.7 us (3%)
  other arithmetic  12.3 us (3%)
    all_gather x1, waiting for transfers between devices, local(): lax.all_gather(value_matrix_rows, 'row', axis=0, tiled=True)  65.1 us
    all_gather x1, waiting for transfers between devices, local(): lax.all_gather(earlier[1], 'row', axis=0, tiled=True)  64.9 us
    all_gather x1, waiting for transfers between devices, local(): lax.all_gather(earlier[0], 'row', axis=0, tiled=True)  32.3 us
    another operation x2, loops' own time, fold_piece(): return lax.fori_loop(0, steps_count, advance, carried)  30.4 us
    all_gather x1, blocking collectives, local(): lax.all_gather(starts_next, 'row', axis=0, tiled=True)  26.8 us
    dot_general x9, matrix products, compute(): jnp.einsum('hgqk,khd->hgqd', weights.astype(jnp.bfloat16), value_part, pr...  24.1 us
    another operation x16, loops' own time, update(): return lax.cond(needed, compute, lambda unchanged: unchanged, carried)  23.4 us
    all_gather x1, blocking collectives, local(): lax.all_gather(earlier[2], 'row', axis=0, tiled=True)  19.4 us
  transfers between devices with their start and end apart: 7, of which 6 were waited for; matrix products, arithmetic and copies ran while one was open for 5% of the time, Pallas kernels for 0%

commit v1 on v0

v1 whole, which is shorter than its diff:
```python
import functools
import math

import jax
import jax.numpy as jnp
from jax import lax
from jax.experimental import pallas as pl
from jax.experimental.pallas import tpu as pltpu
from jax.sharding import PartitionSpec as P

MASKED = -1e30
STAGES = ((0,), (1, 2), (3, 4), (5, 6), (7, 8))
OFFSETS = (1, 3, 2)
CHUNKS = 9
TILE = 512
F32, BF16 = jnp.float32, jnp.bfloat16


def kernel(rows, cols, q_hbm, kv_ref, start_ref, keep_ref, out_hbm,
           kvbuf, kvs, qraw, meta, qbuf, hot, bias, acc, top, ostage,
           one_send, one_recv, two_send, two_recv, mate_send, mate_recv, here):
    block = q_hbm.shape[0]
    per_seg = rows // 2
    ring = per_seg // 2
    row, col = lax.axis_index("row"), lax.axis_index("col")
    core = lax.rem(row, 2)
    other = 1 - core
    place = row // 2
    side = lax.rem(place, 2)
    y = place // 2
    chip = col * per_seg + place
    next_col = lax.rem(col + 1, cols)
    last_col = lax.rem(col + cols - 1, cols)

    def device(seg, at_y, at_side, which):
        return {"row": (at_y * 2 + at_side) * 2 + which, "col": seg}

    mate = device(col, y, side, other)

    def remote(src, dst, send, recv, target):
        return pltpu.make_async_remote_copy(
            src_ref=src, dst_ref=dst, send_sem=send, recv_sem=recv,
            device_id=target, device_id_type=pl.DeviceIdType.MESH)

    def arrived(dst, sem):
        remote(dst, dst, mate_send.at[0], sem, mate).wait_recv()

    barrier = pltpu.get_barrier_semaphore()

    def greet(target):
        pl.semaphore_signal(barrier, inc=1, device_id=target, device_id_type=pl.DeviceIdType.MESH)

    greet(mate)
    for which in (0, 1):
        greet(device(col, y, 1 - side, which))
        greet(device(last_col, y, side, which))
        greet(device(last_col, y, 1 - side, which))
    for offset in OFFSETS:
        greet(device(col, lax.rem(y + offset, ring), side, core))

    def half(which):
        return pl.ds(pl.multiple_of(which * 16, 16), 16)

    own_q = pltpu.make_async_copy(q_hbm.at[:, half(core), :], qraw.at[core], here.at[0])
    own_q.start()

    for which in (0, 1):
        for h in (0, 1):
            kvs[which, 0, h] = kv_ref[which, 0, h].astype(F32).T.astype(BF16)
            kvs[which, 1, h] = kv_ref[which, 1, h]
    own_kv = pltpu.make_async_copy(kvs.at[core], kvbuf.at[0, core], here.at[1])
    own_kv.start()

    backs = [0, 7 - 6 * side, 8]
    slots = [0, 3 - 2 * side, 2]
    for place_at, offset in enumerate(OFFSETS):
        backs += [2 * offset, 2 * offset - 1 + 2 * side]
        slots += [4 + 2 * place_at, 5 + 2 * place_at]

    own_block = chip * 2 + core
    for i in range(CHUNKS):
        for which in (0, 1):
            number = (chip - backs[i]) * 2 + which
            flag = keep_ref[0, jnp.maximum(number, 0)]
            flag = jnp.where(number == own_block, 1, flag)
            line = i * 2 + which
            meta[core, line:line + 1, :] = jnp.full((1, block), flag, jnp.int32)
    line = 2 * CHUNKS
    meta[core, line:line + 1, :] = start_ref[...]

    pl.semaphore_wait(barrier, 10)

    sends = [
        remote(kvs.at[other], kvbuf.at[0, core], mate_send.at[2], mate_recv.at[2], mate),
        remote(meta.at[core], meta.at[core], mate_send.at[0], mate_recv.at[0], mate),
        remote(q_hbm.at[:, half(other), :], qraw.at[core], mate_send.at[1], mate_recv.at[1], mate),
    ]
    for slot, seg, at_side in ((2, next_col, side), (1, col, 1 - side), (3, next_col, 1 - side)):
        for which in (0, 1):
            sends.append(remote(kvs.at[which], kvbuf.at[slot, core],
                                one_send.at[slot - 1, which], one_recv.at[slot - 1, core],
                                device(seg, y, at_side, which)))
    for send in sends:
        send.start()

    def along(i, offset, cross):
        held = y + offset < ring
        source = jnp.where(held, 0, 2) + cross
        to = 4 + 2 * i + cross
        return remote(kvbuf.at[source], kvbuf.at[to], two_send.at[i, cross], two_recv.at[i, cross],
                      device(col, lax.rem(y + offset, ring), side, core))

    group = lax.broadcasted_iota(jnp.int32, hot.shape, 0) // 8
    lane = lax.broadcasted_iota(jnp.int32, hot.shape, 1)
    hot[...] = jnp.where(group == lane, 1.0, 0.0).astype(BF16)

    def make_bias(t):
        starts = jnp.broadcast_to(meta[t, 2 * CHUNKS:2 * CHUNKS + 1, :], (block, block)).T
        key_off = lax.broadcasted_iota(jnp.int32, (block, block), 1)
        query_pos = (chip * 2 + t) * block + lax.broadcasted_iota(jnp.int32, (block, block), 0)
        for i in range(CHUNKS):
            for which in (0, 1):
                key_pos = ((chip - backs[i]) * 2 + which) * block + key_off
                line = i * 2 + which
                flags = meta[t, line:line + 1, :]
                seen = (flags == 1) & (key_pos >= starts) & (key_pos <= query_pos)
                bias[t, i, :, which * block:(which + 1) * block] = (
                    jnp.where(seen, 0.0, MASKED).astype(BF16))

    def regroup(t):
        def piece(i, _):
            at = pl.ds(pl.multiple_of(i * 64, 64), 64)
            raw = qraw[t, at].astype(F32)
            to = pl.ds(pl.multiple_of(i * 512, 512), 512)
            qbuf[t, 0, to, :] = raw[:, :8, :].reshape(512, 128).astype(BF16)
            qbuf[t, 1, to, :] = raw[:, 8:, :].reshape(512, 128).astype(BF16)
            return 0
        lax.fori_loop(0, block // 64, piece, 0)

    scale = 1.0 / math.sqrt(128)
    ones = jnp.ones((2 * block, 128), BF16)
    tiles = block * 8 // TILE

    def run(stage, t):
        first, last = stage == 0, stage == len(STAGES) - 1
        units = [(r, h) for r in range(tiles) for h in (0, 1)]

        def score(r, h):
            at = slice(r * TILE, (r + 1) * TILE)
            lhs = jnp.concatenate([qbuf[t, h, at, :], hot[at, :]], axis=1)
            parts = []
            for i in STAGES[stage]:
                keys = jnp.concatenate([kvbuf[slots[i], 0, 0, h], kvbuf[slots[i], 1, 0, h]], axis=1)
                keys = jnp.concatenate([keys, bias[t, i]], axis=0)
                parts.append(jnp.dot(lhs, keys, preferred_element_type=F32))
            return parts

        done = []
        ready = score(*units[0])
        for n, (r, h) in enumerate(units):
            at = slice(r * TILE, (r + 1) * TILE)
            parts = ready
            if n + 1 < len(units):
                ready = score(*units[n + 1])
            high = functools.reduce(jnp.maximum, parts)
            new_top = jnp.broadcast_to(jnp.max(high, axis=1, keepdims=True), (TILE, 128))
            if not first:
                old_top = top[t, h, at, :]
                new_top = jnp.maximum(old_top, new_top)
            wide_top = jnp.concatenate([new_top, new_top], axis=1)
            total = None
            for i, part in zip(STAGES[stage], parts):
                weights = jnp.exp((part - wide_top) * scale).astype(BF16)
                values = jnp.concatenate([kvbuf[slots[i], 0, 1, h], kvbuf[slots[i], 1, 1, h]], axis=0)
                values = jnp.concatenate([values, ones], axis=1)
                product = jnp.dot(weights, values, preferred_element_type=F32)
                total = product if total is None else total + product
            if not first:
                factor = jnp.exp((old_top - new_top) * scale)
                total = total + acc[t, h, at, :] * jnp.concatenate([factor, factor], axis=1)
            if last:
                done.append((total[:, :128] / total[:, 128:]).reshape(TILE // 8, 8, 128))
                if h == 1:
                    both = jnp.concatenate(done[-2:], axis=1).astype(BF16)
                    ostage[t, r * (TILE // 8):(r + 1) * (TILE // 8)] = both
            else:
                acc[t, h, at, :] = total
                top[t, h, at, :] = new_top

    def run_both(stage):
        def step(t, _):
            run(stage, t)
            return 0
        lax.fori_loop(0, 2, step, 0)

    make_bias(core)
    own_q.wait()
    regroup(core)
    own_kv.wait()
    arrived(kvbuf.at[0, other], mate_recv.at[2])
    for i, offset in enumerate(OFFSETS):
        @pl.when(y + offset < ring)
        def _():
            along(i, offset, 0).start()
    arrived(meta.at[other], mate_recv.at[0])
    arrived(qraw.at[other], mate_recv.at[1])
    make_bias(other)
    regroup(other)
    run_both(0)
    for slot in (2, 1, 3):
        for which in (0, 1):
            arrived(kvbuf.at[slot, which], one_recv.at[slot - 1, which])
    for i, offset in enumerate(OFFSETS):
        @pl.when(y + offset >= ring)
        def _():
            along(i, offset, 0).start()
        along(i, offset, 1).start()
    run_both(1)
    for stage in range(2, 5):
        for cross in (0, 1):
            arrived(kvbuf.at[2 * stage + cross], two_recv.at[stage - 2, cross])
        if stage < 4:
            run_both(stage)

    def finish(t, _):
        t = jnp.where(t == 0, other, core)
        run(4, t)

        @pl.when(t == other)
        def _():
            remote(ostage.at[other], out_hbm.at[:, half(core), :],
                   mate_send.at[3], mate_recv.at[3], mate).start()
        return 0

    lax.fori_loop(0, 2, finish, 0)
    own_out = pltpu.make_async_copy(ostage.at[core], out_hbm.at[:, half(core), :], here.at[0])
    own_out.start()
    for send in sends:
        send.wait_send()
    for i, offset in enumerate(OFFSETS):
        for cross in (0, 1):
            along(i, offset, cross).wait_send()
    own_out.wait()
    remote(ostage.at[other], out_hbm.at[:, half(core), :],
           mate_send.at[3], mate_recv.at[3], mate).wait_send()
    arrived(out_hbm.at[:, half(other), :], mate_recv.at[3])


def local(queries, rotated_key_rows, value_matrix_rows, doc_start, block_keep):
    block = queries.shape[0]
    rows, cols = lax.axis_size("row"), lax.axis_size("col")
    kv = jnp.stack([rotated_key_rows, value_matrix_rows])
    kv = kv.reshape(2, block, 2, 2, 128).transpose(2, 0, 3, 1, 4)
    vmem = pl.BlockSpec(memory_space=pltpu.VMEM)
    hbm = pl.BlockSpec(memory_space=pl.ANY)
    return pl.pallas_call(
        functools.partial(kernel, rows, cols),
        out_shape=jax.ShapeDtypeStruct(queries.shape, BF16),
        in_specs=[hbm, vmem, vmem, pl.BlockSpec(memory_space=pltpu.SMEM)],
        out_specs=hbm,
        scratch_shapes=[
            pltpu.VMEM((10, 2, 2, 2, block, 128), BF16),
            pltpu.VMEM((2, 2, 2, block, 128), BF16),
            pltpu.VMEM((2, block, 16, 128), BF16),
            pltpu.VMEM((2, 24, 128), jnp.int32),
            pltpu.VMEM((2, 2, block * 8, 128), BF16),
            pltpu.VMEM((block * 8, 128), BF16),
            pltpu.VMEM((2, CHUNKS, block, 2 * block), BF16),
            pltpu.VMEM((2, 2, block * 8, 256), F32),
            pltpu.VMEM((2, 2, block * 8, 128), F32),
            pltpu.VMEM((2, block, 16, 128), BF16),
            pltpu.SemaphoreType.DMA((3, 2)),
            pltpu.SemaphoreType.DMA((3, 2)),
            pltpu.SemaphoreType.DMA((3, 2)),
            pltpu.SemaphoreType.DMA((3, 2)),
            pltpu.SemaphoreType.DMA((4,)),
            pltpu.SemaphoreType.DMA((4,)),
            pltpu.SemaphoreType.DMA((2,)),
        ],
        compiler_params=pltpu.CompilerParams(
            collective_id=0, has_side_effects=True, vmem_limit_bytes=48 * 1024 * 1024),
        cost_estimate=pl.CostEstimate(flops=10**10, bytes_accessed=8 * 10**6, transcendentals=10**7),
    )(queries, kv, doc_start.reshape(1, block), block_keep)


def solution(mesh):
    return jax.shard_map(
        local,
        mesh=mesh,
        in_specs=(
            P(("col", "row"), None, None),
            P(("col", "row"), None, None),
            P(("col", "row"), None, None),
            P(("col", "row")),
            P(("col", "row"), None),
        ),
        out_specs=P(("col", "row"), None, None),
        check_vma=False,
    )
```

time: 377 us -> 67.2 us (0.18)
  waiting for transfers between devices: 169 us -> 0 us
  Pallas kernels: 0 us -> 63.4 us
  loops' own time: 53.8 us -> 0 us
  blocking collectives: 46.2 us -> 0 us
  matrix products: 39.3 us -> 0 us
  local copies, waits for them, and re-layouts: 28.8 us -> 3.54 us
  between operations: 13.3 us -> 0.05 us
  starting transfers between devices: 12.7 us -> 0 us
  other arithmetic: 12.3 us -> 0.03 us
    all_gather x4 -> x0, waiting for transfers between devices: 165 us -> none  [the longest x1 65.1 us: local(): lax.all_gather(value_matrix_rows, 'row', axis=0, tiled=True)]
    pallas_call x0 -> x1, Pallas kernels: none -> 63.4 us  [local(): pl.pallas_call(functools.partial(kernel, rows, cols), out_shape=jax.Shape...]
    another operation x18 -> x0, loops' own time: 53.8 us -> none  [the longest x2 30.4 us: fold_piece(): return lax.fori_loop(0, steps_count, advance, carried)]
    all_gather x2 -> x0, blocking collectives: 46.2 us -> none  [the longest x1 26.8 us: local(): lax.all_gather(starts_next, 'row', axis=0, tiled=True)]
    dot_general x18 -> x0, matrix products: 39.3 us -> none  [the longest x9 24.1 us: compute(): jnp.einsum('hgqk,khd->hgqd', weights.astype(jnp.bfloat16), value_part, pr...]
    slice x32 -> x0, local copies, waits for them, and re-layouts: 19.4 us -> none  [the longest x16 9.74 us: update(): key_pos[-1] > query_pos[0] - doc_reach]
    ppermute x3 -> x0, starting transfers between devices: 12.6 us -> none  [from_behind(): return lax.ppermute(array, axis, pairs)]
    reduce_sum x9 -> x0, other arithmetic: 8.1 us -> none  [compute(): weight_total = weight_total * factor + jnp.sum(weights, axis=-1)]
  transfers between devices with their start and end apart: 7 -> 0, of which waited for: 6 -> 0; matrix products, arithmetic and copies ran while one was open for 5% -> 0% of each run, Pallas kernels for 0% -> 0%
where the time goes in v1:
time: 67.2 us; the launch traced here: 67 us
  Pallas kernels  63.4 us (94%)
  local copies, waits for them, and re-layouts  3.54 us (5%)
    pallas_call x1, Pallas kernels, local(): pl.pallas_call(functools.partial(kernel, rows, cols), out_shape=jax.Shape...  63.4 us
    unnamed x9, local copies, waits for them, and re-layouts  3.54 us

profile of v1, /device:TPU:1, one launch (start us, length us, event | category | flops | bytes accessed | tf_op | source)
XLA Modules:
  0.0 67.0 jit_solution(14718945540138157184)
XLA Ops:
  0.0 0.0 copy-start
  0.0 1.0 %copy.6 = bf16[128,4,128]{2,0,1:T(8,128)(2,1)S(1)} copy(bf16[128,4,128]{2,1,0:T(4,128)(2,1)} %param.6) | data formatting | bytes 262144 | tf_op args[1]
  1.0 0.9 %copy.7 = bf16[128,4,128]{2,0,1:T(8,128)(2,1)S(1)} copy(bf16[128,4,128]{2,1,0:T(4,128)(2,1)} %param.7) | data formatting | bytes 262144 | tf_op args[2]
  1.9 0.0 copy-start.1
  2.0 0.0 copy-start.2
  2.0 0.0 copy-done
  2.0 0.6 copy-done.1
  2.6 0.0 copy-done.2
  2.6 63.4 %shard_map.55 = bf16[128,32,128]{2,1,0:T(8,128)(2,1)S(1)} custom-call(bf16[128,32,128]{2,1,0:T(8,128)(2,1)S(1)} %copy-done, bf16[2,2,2,128,128]{4,3,2,1,0:T(8,128)(2,1)S(1)} %maximum_bitcast_fusion.kv_ref, s32[1,128]{1,0:T(1,128)S(1)} %bitcast.5, s32[1,512]{1,0:T(1,128)S(1)} %copy-done.1), custom_call_target="tpu_custom_call" | custom-call | flops 10000000000 | bytes 8000000 | tf_op jit(solution)/shard_map/pallas_call | solution.py:256
  66.1 1.0 %copy.9 = bf16[128,32,128]{2,1,0:T(8,128)(2,1)} copy(bf16[128,32,128]{2,1,0:T(8,128)(2,1)S(1)} %shard_map.55) | data formatting | bytes 2097152
  (1 shorter events, 0.0 us)
Async XLA Ops:
  0.0 2.0 %copy-start = (bf16[128,32,128]{2,1,0:T(8,128)(2,1)S(1)}, bf16[128,32,128]{2,1,0:T(8,128)(2,1)}, u32[]{:S(2)}) copy-start(bf16[128,32,128]{2,1,0:T(8,128)(2,1)} %q_hbm.1) | copy-start | bytes 3145732
  1.9 0.7 %copy-start.1 = (s32[1,512]{1,0:T(1,128)S(1)}, s32[1,512]{1,0:T(1,128)}, u32[]{:S(2)}) copy-start(s32[1,512]{1,0:T(1,128)} %keep_ref.1) | copy-start | bytes 6148
  2.0 0.7 %copy-start.2 = (s32[128]{0:T(128)S(1)}, s32[128]{0:T(128)}, u32[]{:S(2)}) copy-start(s32[128]{0:T(128)} %param.8) | copy-start | bytes 1540

commit v2 on v1

v2 whole, which is shorter than its diff:
```python
import functools
import math

import jax
import jax.numpy as jnp
from jax import lax
from jax.experimental import pallas as pl
from jax.experimental.pallas import tpu as pltpu
from jax.sharding import PartitionSpec as P

MASKED = -1e30
STAGES = ((0,), (1, 2), (3, 4), (5, 6), (7, 8))
OFFSETS = (1, 3, 2)
X_TRANSIT, Y_TRANSIT = 10, 11
CHUNKS = 9
TILE = 512
F32, BF16 = jnp.float32, jnp.bfloat16


def kernel(rows, cols, q_hbm, kv_ref, start_ref, keep_ref, out_hbm,
           kvbuf, kvs, qraw, meta, qbuf, hot, bias, acc, top, ostage,
           one_send, one_recv, two_send, two_recv, pass_send, pass_recv,
           mate_send, mate_recv, here):
    block = q_hbm.shape[0]
    per_seg = rows // 2
    ring = per_seg // 2
    row, col = lax.axis_index("row"), lax.axis_index("col")
    core = lax.rem(row, 2)
    other = 1 - core
    place = row // 2
    side = lax.rem(place, 2)
    y = place // 2
    chip = col * per_seg + place
    next_col = lax.rem(col + 1, cols)
    last_col = lax.rem(col + cols - 1, cols)

    def device(seg, at_y, at_side, which):
        return {"row": (at_y * 2 + at_side) * 2 + which, "col": seg}

    mate = device(col, y, side, other)

    def beside(step, which):
        x = lax.rem(side * 2 + lax.rem(col, 2) + step + 4, 4)
        return device(col - lax.rem(col, 2) + lax.rem(x, 2), y, x // 2, which)

    def above(step):
        return device(col, lax.rem(y + step + ring, ring), side, core)

    way = 1 - 2 * core

    def remote(src, dst, send, recv, target):
        return pltpu.make_async_remote_copy(
            src_ref=src, dst_ref=dst, send_sem=send, recv_sem=recv,
            device_id=target, device_id_type=pl.DeviceIdType.MESH)

    def arrived(dst, sem):
        remote(dst, dst, mate_send.at[0], sem, mate).wait_recv()

    barrier = pltpu.get_barrier_semaphore()

    def greet(target):
        pl.semaphore_signal(barrier, inc=1, device_id=target, device_id_type=pl.DeviceIdType.MESH)

    greet(mate)
    for which in (0, 1):
        greet(beside(-way, which))

    @pl.when(col > 0)
    def _():
        for which in (0, 1):
            greet(device(last_col, y, side, which))
            greet(device(last_col, y, 1 - side, which))

    @pl.when(col == 0)
    def _():
        kvbuf[2:4] = jnp.zeros((2,) + kvbuf.shape[1:], BF16)

    greet(above(1))
    greet(above(-1))

    def half(which):
        return pl.ds(pl.multiple_of(which * 16, 16), 16)

    own_q = pltpu.make_async_copy(q_hbm.at[:, half(core), :], qraw.at[core], here.at[0])
    own_q.start()

    for which in (0, 1):
        for h in (0, 1):
            kvs[which, 0, h] = kv_ref[which, 0, h]
            kvs[which, 1, h] = kv_ref[which, 1, h].astype(F32).T.astype(BF16)
    own_kv = pltpu.make_async_copy(kvs.at[core], kvbuf.at[0, core], here.at[1])
    own_kv.start()

    backs = [0, 7 - 6 * side, 8]
    slots = [0, 3 - 2 * side, 2]
    for place_at, offset in enumerate(OFFSETS):
        backs += [2 * offset, 2 * offset - 1 + 2 * side]
        slots += [4 + 2 * place_at, 5 + 2 * place_at]

    own_block = chip * 2 + core
    for i in range(CHUNKS):
        for which in (0, 1):
            number = (chip - backs[i]) * 2 + which
            flag = keep_ref[0, jnp.maximum(number, 0)]
            flag = jnp.where(number == own_block, 1, flag)
            line = i * 2 + which
            meta[core, line:line + 1, :] = jnp.full((1, block), flag, jnp.int32)
    line = 2 * CHUNKS
    meta[core, line:line + 1, :] = start_ref[...]

    pl.semaphore_wait(barrier, jnp.where(col < cols - 1, 9, 5))

    sends = [
        remote(kvs.at[other], kvbuf.at[0, core], mate_send.at[2], mate_recv.at[2], mate),
        remote(meta.at[core], meta.at[core], mate_send.at[0], mate_recv.at[0], mate),
        remote(q_hbm.at[:, half(other), :], qraw.at[core], mate_send.at[1], mate_recv.at[1], mate),
    ]
    for which in (0, 1):
        sends.append(remote(kvs.at[which], kvbuf.at[X_TRANSIT, core],
                            one_send.at[0, which], one_recv.at[0, core],
                            beside(1 - 2 * which, which)))
    onward = []
    for slot, at_side in ((2, side), (3, 1 - side)):
        for which in (0, 1):
            onward.append(remote(kvs.at[which], kvbuf.at[slot, core],
                                 one_send.at[slot - 1, which], one_recv.at[slot - 1, core],
                                 device(next_col, y, at_side, which)))
    for send in sends:
        send.start()

    @pl.when(col < cols - 1)
    def _():
        for send in onward:
            send.start()

    def along(i, cross):
        offset = OFFSETS[i]
        held = y + offset < ring
        source = jnp.where(held, 0, 2) + cross
        to = (Y_TRANSIT if offset == 2 else 4 + 2 * i) + cross
        target = above(way) if offset == 2 else above(1 if offset == 1 else -1)
        return remote(kvbuf.at[source], kvbuf.at[to], two_send.at[i, cross], two_recv.at[i, cross],
                      target)

    pass_x = remote(kvbuf.at[X_TRANSIT], kvbuf.at[1], pass_send.at[0], pass_recv.at[0],
                    beside(way, core))
    pass_y = [remote(kvbuf.at[Y_TRANSIT + cross], kvbuf.at[8 + cross],
                     pass_send.at[1 + cross], pass_recv.at[1 + cross], above(way))
              for cross in (0, 1)]

    group = lax.broadcasted_iota(jnp.int32, hot.shape, 1) // 8
    token = lax.broadcasted_iota(jnp.int32, hot.shape, 0)
    hot[...] = jnp.where(group == token, 1.0, 0.0).astype(BF16)

    def make_bias(t):
        starts = meta[t, 2 * CHUNKS:2 * CHUNKS + 1, :]
        key_off = lax.broadcasted_iota(jnp.int32, (block, block), 0)
        query_pos = (chip * 2 + t) * block + lax.broadcasted_iota(jnp.int32, (block, block), 1)
        for i in range(CHUNKS):
            for which in (0, 1):
                key_pos = ((chip - backs[i]) * 2 + which) * block + key_off
                line = i * 2 + which
                flags = meta[t, line:line + 1, :]
                seen = (flags == 1) & (key_pos >= starts) & (key_pos <= query_pos)
                bias[t, i, which * block:(which + 1) * block, :] = (
                    jnp.where(seen, 0.0, MASKED).astype(BF16))

    def regroup(t):
        def piece(i, _):
            at = pl.ds(pl.multiple_of(i * 64, 64), 64)
            raw = qraw[t, at].astype(F32)
            to = pl.ds(pl.multiple_of(i * 512, 512), 512)
            qbuf[t, 0, :, to] = raw[:, :8, :].reshape(512, 128).T.astype(BF16)
            qbuf[t, 1, :, to] = raw[:, 8:, :].reshape(512, 128).T.astype(BF16)
            return 0
        lax.fori_loop(0, block // 64, piece, 0)

    scale = 1.0 / math.sqrt(128)
    tiles = block * 8 // TILE

    def run(stage, t):
        first, last = stage == 0, stage == len(STAGES) - 1
        used = STAGES[stage]
        ones = jnp.ones((16, len(used) * 2 * block), BF16)
        units = [(r, h) for r in range(tiles) for h in (0, 1)]

        def score(r, h):
            at = slice(r * TILE, (r + 1) * TILE)
            rhs = jnp.concatenate([qbuf[t, h, :, at], hot[:, at]], axis=0)
            keys = jnp.concatenate(
                [kvbuf[slots[i], which, 0, h] for i in used for which in (0, 1)], axis=0)
            masks = jnp.concatenate([bias[t, i] for i in used], axis=0)
            return jnp.dot(jnp.concatenate([keys, masks], axis=1), rhs, preferred_element_type=F32)

        done = []
        ready = score(*units[0])
        for n, (r, h) in enumerate(units):
            at = slice(r * TILE, (r + 1) * TILE)
            scores = ready
            if n + 1 < len(units):
                ready = score(*units[n + 1])
            new_top = jnp.max(scores, axis=0, keepdims=True)
            if not first:
                old_top = top[t, h, 0:1, at]
                new_top = jnp.maximum(old_top, new_top)
            weights = jnp.exp((scores - new_top) * scale).astype(BF16)
            values = jnp.concatenate(
                [kvbuf[slots[i], which, 1, h] for i in used for which in (0, 1)], axis=1)
            total = jnp.dot(jnp.concatenate([values, ones], axis=0), weights,
                            preferred_element_type=F32)
            if not first:
                total = total + acc[t, h, :, at] * jnp.exp((old_top - new_top) * scale)
            if last:
                result = total[:128] / total[128:129]
                done.append(result.T.reshape(TILE // 8, 8, 128))
                if h == 1:
                    both = jnp.concatenate(done[-2:], axis=1).astype(BF16)
                    ostage[t, r * (TILE // 8):(r + 1) * (TILE // 8)] = both
            else:
                acc[t, h, :, at] = total
                top[t, h, 0:1, at] = new_top

    def run_both(stage, between=None):
        def step(t, _):
            run(stage, t)
            if between is not None:
                @pl.when(t == 0)
                def _():
                    between()
            return 0
        lax.fori_loop(0, 2, step, 0)

    def start_own(early):
        for i in (2, 0, 1):
            held = y + OFFSETS[i] < ring

            @pl.when(held if early else jnp.logical_not(held))
            def _():
                along(i, 0).start()

    def hand_on(cross):
        arrived(kvbuf.at[Y_TRANSIT + cross], two_recv.at[2, cross])
        pass_y[cross].start()

    def before(slot):
        @pl.when(col > 0)
        def _():
            for which in (0, 1):
                arrived(kvbuf.at[slot, which], one_recv.at[slot - 1, which])

    def previous():
        before(2)
        start_own(False)

    make_bias(core)
    own_q.wait()
    regroup(core)
    own_kv.wait()
    arrived(kvbuf.at[0, other], mate_recv.at[2])
    start_own(True)
    arrived(meta.at[other], mate_recv.at[0])
    arrived(qraw.at[other], mate_recv.at[1])
    make_bias(other)
    regroup(other)
    for which in (0, 1):
        arrived(kvbuf.at[X_TRANSIT, which], one_recv.at[0, which])
    pass_x.start()
    run_both(0, previous)
    arrived(kvbuf.at[1], pass_recv.at[0])
    before(3)
    for i in (2, 0, 1):
        along(i, 1).start()
    run_both(1, lambda: hand_on(0))
    hand_on(1)
    for stage in (2, 3):
        for cross in (0, 1):
            arrived(kvbuf.at[2 * stage + cross], two_recv.at[stage - 2, cross])
        run_both(stage)
    for cross in (0, 1):
        arrived(kvbuf.at[8 + cross], pass_recv.at[1 + cross])

    def finish(t, _):
        t = jnp.where(t == 0, other, core)
        run(4, t)

        @pl.when(t == other)
        def _():
            remote(ostage.at[other], out_hbm.at[:, half(core), :],
                   mate_send.at[3], mate_recv.at[3], mate).start()
        return 0

    lax.fori_loop(0, 2, finish, 0)
    own_out = pltpu.make_async_copy(ostage.at[core], out_hbm.at[:, half(core), :], here.at[0])
    own_out.start()
    for send in sends:
        send.wait_send()

    @pl.when(col < cols - 1)
    def _():
        for send in onward:
            send.wait_send()

    for i in range(3):
        for cross in (0, 1):
            along(i, cross).wait_send()
    pass_x.wait_send()
    for copy in pass_y:
        copy.wait_send()
    own_out.wait()
    remote(ostage.at[other], out_hbm.at[:, half(core), :],
           mate_send.at[3], mate_recv.at[3], mate).wait_send()
    arrived(out_hbm.at[:, half(other), :], mate_recv.at[3])


def local(queries, rotated_key_rows, value_matrix_rows, doc_start, block_keep):
    block = queries.shape[0]
    rows, cols = lax.axis_size("row"), lax.axis_size("col")
    kv = jnp.stack([rotated_key_rows, value_matrix_rows])
    kv = kv.reshape(2, block, 2, 2, 128).transpose(2, 0, 3, 1, 4)
    vmem = pl.BlockSpec(memory_space=pltpu.VMEM)
    hbm = pl.BlockSpec(memory_space=pl.ANY)
    return pl.pallas_call(
        functools.partial(kernel, rows, cols),
        out_shape=jax.ShapeDtypeStruct(queries.shape, BF16),
        in_specs=[hbm, vmem, vmem, pl.BlockSpec(memory_space=pltpu.SMEM)],
        out_specs=hbm,
        scratch_shapes=[
            pltpu.VMEM((13, 2, 2, 2, block, 128), BF16),
            pltpu.VMEM((2, 2, 2, block, 128), BF16),
            pltpu.VMEM((2, block, 16, 128), BF16),
            pltpu.VMEM((2, 24, 128), jnp.int32),
            pltpu.VMEM((2, 2, 128, block * 8), BF16),
            pltpu.VMEM((block, block * 8), BF16),
            pltpu.VMEM((2, CHUNKS, 2 * block, block), BF16),
            pltpu.VMEM((2, 2, 144, block * 8), F32),
            pltpu.VMEM((2, 2, 8, block * 8), F32),
            pltpu.VMEM((2, block, 16, 128), BF16),
            pltpu.SemaphoreType.DMA((3, 2)),
            pltpu.SemaphoreType.DMA((3, 2)),
            pltpu.SemaphoreType.DMA((3, 2)),
            pltpu.SemaphoreType.DMA((3, 2)),
            pltpu.SemaphoreType.DMA((3,)),
            pltpu.SemaphoreType.DMA((3,)),
            pltpu.SemaphoreType.DMA((4,)),
            pltpu.SemaphoreType.DMA((4,)),
            pltpu.SemaphoreType.DMA((2,)),
        ],
        compiler_params=pltpu.CompilerParams(
            collective_id=0, has_side_effects=True, vmem_limit_bytes=48 * 1024 * 1024),
        cost_estimate=pl.CostEstimate(flops=10**10, bytes_accessed=8 * 10**6, transcendentals=10**7),
    )(queries, kv, doc_start.reshape(1, block), block_keep)


def solution(mesh):
    return jax.shard_map(
        local,
        mesh=mesh,
        in_specs=(
            P(("col", "row"), None, None),
            P(("col", "row"), None, None),
            P(("col", "row"), None, None),
            P(("col", "row")),
            P(("col", "row"), None),
        ),
        out_specs=P(("col", "row"), None, None),
        check_vma=False,
    )
```

time: 67.2 us -> 50.2 us (0.75)
  the two profiles are of different devices: /device:TPU:1 before, /device:TPU:2 now
where the time goes in v2:
time: 50.2 us; the launch traced here: 50 us
  Pallas kernels  46.4 us (92%)
  local copies, waits for them, and re-layouts  3.54 us (7%)
    pallas_call x1, Pallas kernels, local(): pl.pallas_call(functools.partial(kernel, rows, cols), out_shape=jax.Shape...  46.4 us
    unnamed x9, local copies, waits for them, and re-layouts  3.54 us

profile of v2, /device:TPU:2, one launch (start us, length us, event | category | flops | bytes accessed | tf_op | source)
XLA Modules:
  0.0 50.0 jit_solution(13454368145595310013)
XLA Ops:
  0.0 0.0 copy-start
  0.0 1.0 %copy.6 = bf16[128,4,128]{2,0,1:T(8,128)(2,1)S(1)} copy(bf16[128,4,128]{2,1,0:T(4,128)(2,1)} %param.6) | data formatting | bytes 262144 | tf_op args[1]
  1.0 0.9 %copy.7 = bf16[128,4,128]{2,0,1:T(8,128)(2,1)S(1)} copy(bf16[128,4,128]{2,1,0:T(4,128)(2,1)} %param.7) | data formatting | bytes 262144 | tf_op args[2]
  1.9 0.0 copy-start.1
  2.0 0.0 copy-start.2
  2.0 0.0 copy-done
  2.0 0.6 %copy-done.1 = s32[1,512]{1,0:T(1,128)S(1)} copy-done((s32[1,512]{1,0:T(1,128)S(1)}, s32[1,512]{1,0:T(1,128)}, u32[]{:S(2)}) %copy-start.1) | copy-done | bytes 2072
  2.6 0.0 copy-done.2
  2.6 46.4 %shard_map.55 = bf16[128,32,128]{2,1,0:T(8,128)(2,1)S(1)} custom-call(bf16[128,32,128]{2,1,0:T(8,128)(2,1)S(1)} %copy-done, bf16[2,2,2,128,128]{4,3,2,1,0:T(8,128)(2,1)S(1)} %maximum_bitcast_fusion.kv_ref, s32[1,128]{1,0:T(1,128)S(1)} %bitcast.5, s32[1,512]{1,0:T(1,128)S(1)} %copy-done.1), custom_call_target="tpu_custom_call" | custom-call | flops 10000000000 | bytes 8000000 | tf_op jit(solution)/shard_map/pallas_call | solution.py:322
  49.1 1.0 %copy.9 = bf16[128,32,128]{2,1,0:T(8,128)(2,1)} copy(bf16[128,32,128]{2,1,0:T(8,128)(2,1)S(1)} %shard_map.55) | data formatting | bytes 2097152
  (1 shorter events, 0.0 us)
Async XLA Ops:
  0.0 2.0 %copy-start = (bf16[128,32,128]{2,1,0:T(8,128)(2,1)S(1)}, bf16[128,32,128]{2,1,0:T(8,128)(2,1)}, u32[]{:S(2)}) copy-start(bf16[128,32,128]{2,1,0:T(8,128)(2,1)} %q_hbm.1) | copy-start | bytes 3145732
  1.9 0.7 %copy-start.1 = (s32[1,512]{1,0:T(1,128)S(1)}, s32[1,512]{1,0:T(1,128)}, u32[]{:S(2)}) copy-start(s32[1,512]{1,0:T(1,128)} %keep_ref.1) | copy-start | bytes 6148
  2.0 0.7 %copy-start.2 = (s32[128]{0:T(128)S(1)}, s32[128]{0:T(128)}, u32[]{:S(2)}) copy-start(s32[128]{0:T(128)} %param.8) | copy-start | bytes 1540

commit v3 on v2

--- a/solution.py
+++ b/solution.py
@@ -9,16 +9,16 @@
 from jax.sharding import PartitionSpec as P
 
 MASKED = -1e30
-STAGES = ((0,), (1, 2), (3, 4), (5, 6), (7, 8))
+STAGES = ((0,), (1, 2), (3, 5), (7, 4), (6, 8))
 OFFSETS = (1, 3, 2)
-X_TRANSIT, Y_TRANSIT = 10, 11
+X_TRANSIT, Y_TRANSIT, LATE_TRANSIT = 10, 11, 12
 CHUNKS = 9
 TILE = 512
 F32, BF16 = jnp.float32, jnp.bfloat16
 
 
-def kernel(rows, cols, q_hbm, kv_ref, start_ref, keep_ref, out_hbm,
-           kvbuf, kvs, qraw, meta, qbuf, hot, bias, acc, top, ostage,
+def kernel(rows, cols, q_hbm, k_hbm, v_hbm, start_ref, keep_ref, out_hbm,
+           kvbuf, kvs, kvraw, qraw, meta, qbuf, hot, bias, acc, top, ostage,
            one_send, one_recv, two_send, two_recv, pass_send, pass_recv,
            mate_send, mate_recv, here):
     block = q_hbm.shape[0]
@@ -56,6 +56,10 @@
     def arrived(dst, sem):
         remote(dst, dst, mate_send.at[0], sem, mate).wait_recv()
 
+    own_raw = [pltpu.make_async_copy(k_hbm, kvraw.at[0], here.at[1]),
+               pltpu.make_async_copy(v_hbm, kvraw.at[1], here.at[2])]
+    for copy in own_raw:
+        copy.start()
     barrier = pltpu.get_barrier_semaphore()
 
     def greet(target):
@@ -84,10 +88,13 @@
     own_q = pltpu.make_async_copy(q_hbm.at[:, half(core), :], qraw.at[core], here.at[0])
     own_q.start()
 
+    for copy in own_raw:
+        copy.wait()
+    all_keys, all_values = kvraw[0].astype(F32), kvraw[1].astype(F32)
     for which in (0, 1):
         for h in (0, 1):
-            kvs[which, 0, h] = kv_ref[which, 0, h]
-            kvs[which, 1, h] = kv_ref[which, 1, h].astype(F32).T.astype(BF16)
+            kvs[which, 0, h] = all_keys[:, 2 * which + h, :].astype(BF16)
+            kvs[which, 1, h] = all_values[:, 2 * which + h, :].T.astype(BF16)
     own_kv = pltpu.make_async_copy(kvs.at[core], kvbuf.at[0, core], here.at[1])
     own_kv.start()
 
@@ -144,9 +151,11 @@
 
     pass_x = remote(kvbuf.at[X_TRANSIT], kvbuf.at[1], pass_send.at[0], pass_recv.at[0],
                     beside(way, core))
-    pass_y = [remote(kvbuf.at[Y_TRANSIT + cross], kvbuf.at[8 + cross],
-                     pass_send.at[1 + cross], pass_recv.at[1 + cross], above(way))
-              for cross in (0, 1)]
+    pass_y = remote(kvbuf.at[Y_TRANSIT], kvbuf.at[8], pass_send.at[1], pass_recv.at[1], above(way))
+    late = remote(kvbuf.at[8], kvbuf.at[LATE_TRANSIT], two_send.at[2, 1], two_recv.at[2, 1],
+                  beside(way, core))
+    pass_late = remote(kvbuf.at[LATE_TRANSIT], kvbuf.at[9], pass_send.at[2], pass_recv.at[2],
+                       beside(way, core))
 
     group = lax.broadcasted_iota(jnp.int32, hot.shape, 1) // 8
     token = lax.broadcasted_iota(jnp.int32, hot.shape, 0)
@@ -238,9 +247,17 @@
             def _():
                 along(i, 0).start()
 
-    def hand_on(cross):
-        arrived(kvbuf.at[Y_TRANSIT + cross], two_recv.at[2, cross])
-        pass_y[cross].start()
+    def far():
+        arrived(kvbuf.at[Y_TRANSIT], two_recv.at[2, 0])
+        pass_y.start()
+
+    def far_here():
+        arrived(kvbuf.at[8], pass_recv.at[1])
+        late.start()
+
+    def far_on():
+        arrived(kvbuf.at[LATE_TRANSIT], two_recv.at[2, 1])
+        pass_late.start()
 
     def before(slot):
         @pl.when(col > 0)
@@ -268,16 +285,16 @@
     run_both(0, previous)
     arrived(kvbuf.at[1], pass_recv.at[0])
     before(3)
-    for i in (2, 0, 1):
+    for i in (0, 1):
         along(i, 1).start()
-    run_both(1, lambda: hand_on(0))
-    hand_on(1)
-    for stage in (2, 3):
-        for cross in (0, 1):
-            arrived(kvbuf.at[2 * stage + cross], two_recv.at[stage - 2, cross])
-        run_both(stage)
-    for cross in (0, 1):
-        arrived(kvbuf.at[8 + cross], pass_recv.at[1 + cross])
+    run_both(1, far)
+    for i in (0, 1):
+        arrived(kvbuf.at[4 + 2 * i], two_recv.at[i, 0])
+    run_both(2, far_here)
+    arrived(kvbuf.at[5], two_recv.at[0, 1])
+    run_both(3, far_on)
+    arrived(kvbuf.at[7], two_recv.at[1, 1])
+    arrived(kvbuf.at[9], pass_recv.at[2])
 
     def finish(t, _):
         t = jnp.where(t == 0, other, core)
@@ -301,10 +318,10 @@
             send.wait_send()
 
     for i in range(3):
-        for cross in (0, 1):
-            along(i, cross).wait_send()
-    pass_x.wait_send()
-    for copy in pass_y:
+        along(i, 0).wait_send()
+        if i < 2:
+            along(i, 1).wait_send()
+    for copy in (pass_x, pass_y, late, pass_late):
         copy.wait_send()
     own_out.wait()
     remote(ostage.at[other], out_hbm.at[:, half(core), :],
@@ -315,18 +332,17 @@
 def local(queries, rotated_key_rows, value_matrix_rows, doc_start, block_keep):
     block = queries.shape[0]
     rows, cols = lax.axis_size("row"), lax.axis_size("col")
-    kv = jnp.stack([rotated_key_rows, value_matrix_rows])
-    kv = kv.reshape(2, block, 2, 2, 128).transpose(2, 0, 3, 1, 4)
     vmem = pl.BlockSpec(memory_space=pltpu.VMEM)
     hbm = pl.BlockSpec(memory_space=pl.ANY)
     return pl.pallas_call(
         functools.partial(kernel, rows, cols),
         out_shape=jax.ShapeDtypeStruct(queries.shape, BF16),
-        in_specs=[hbm, vmem, vmem, pl.BlockSpec(memory_space=pltpu.SMEM)],
-        out_specs=hbm,
+        in_specs=[hbm, hbm, hbm, vmem, pl.BlockSpec(memory_space=pltpu.SMEM)],
+        out_specs=pl.BlockSpec(memory_space=pl.ANY),
         scratch_shapes=[
             pltpu.VMEM((13, 2, 2, 2, block, 128), BF16),
             pltpu.VMEM((2, 2, 2, block, 128), BF16),
+            pltpu.VMEM((2, block, 4, 128), BF16),
             pltpu.VMEM((2, block, 16, 128), BF16),
             pltpu.VMEM((2, 24, 128), jnp.int32),
             pltpu.VMEM((2, 2, 128, block * 8), BF16),
@@ -343,12 +359,12 @@
             pltpu.SemaphoreType.DMA((3,)),
             pltpu.SemaphoreType.DMA((4,)),
             pltpu.SemaphoreType.DMA((4,)),
-            pltpu.SemaphoreType.DMA((2,)),
+            pltpu.SemaphoreType.DMA((3,)),
         ],
         compiler_params=pltpu.CompilerParams(
-            collective_id=0, has_side_effects=True, vmem_limit_bytes=48 * 1024 * 1024),
+            collective_id=0, has_side_effects=True, vmem_limit_bytes=63 * 1024 * 1024),
         cost_estimate=pl.CostEstimate(flops=10**10, bytes_accessed=8 * 10**6, transcendentals=10**7),
-    )(queries, kv, doc_start.reshape(1, block), block_keep)
+    )(queries, rotated_key_rows, value_matrix_rows, doc_start.reshape(1, block), block_keep)
 
 
 def solution(mesh):

time: 50.2 us -> 52.7 us (1.050)
  the two profiles are of different devices: /device:TPU:2 before, /device:TPU:96 now
where the time goes in v3:
time: 52.7 us; the launch traced here: 52.5 us
  Pallas kernels  50.2 us (95%)
  local copies, waits for them, and re-layouts  2.26 us (4%)
    pallas_call x1, Pallas kernels, local(): pl.pallas_call(functools.partial(kernel, rows, cols), out_shape=jax.Shape...  50.2 us
    unnamed x1, local copies, waits for them, and re-layouts  2.26 us

profile of v3, /device:TPU:96, one launch (start us, length us, event | category | flops | bytes accessed | tf_op | source)
XLA Modules:
  0.0 52.5 jit_solution(12580657220603706929)
XLA Ops:
  0.0 50.2 %shard_map.55 = bf16[128,32,128]{2,1,0:T(8,128)(2,1)} custom-call(bf16[128,32,128]{2,1,0:T(8,128)(2,1)} %q_hbm.1, bf16[128,4,128]{2,1,0:T(4,128)(2,1)} %k_hbm.1, bf16[128,4,128]{2,1,0:T(4,128)(2,1)} %v_hbm.1, s32[1,128]{1,0:T(1,128)} %bitcast.1, s32[1,512]{1,0:T(1,128)} %keep_ref.1), custom_call_target="tpu_custom_call" | custom-call | flops 10000000000 | bytes 8000000 | tf_op jit(solution)/shard_map/pallas_call | solution.py:337
  50.2 2.3 %copy.7 = bf16[128,32,128]{2,1,0:T(8,128)(2,1)} copy(bf16[128,32,128]{2,1,0:T(8,128)(2,1)} %shard_map.55) | data formatting | bytes 2097152

commit v4 on v2

--- a/solution.py
+++ b/solution.py
@@ -9,11 +9,11 @@
 from jax.sharding import PartitionSpec as P
 
 MASKED = -1e30
-STAGES = ((0,), (1, 2), (3, 4), (5, 6), (7, 8))
 OFFSETS = (1, 3, 2)
 X_TRANSIT, Y_TRANSIT = 10, 11
 CHUNKS = 9
-TILE = 512
+TILE = 256
+TOGETHER = 2
 F32, BF16 = jnp.float32, jnp.bfloat16
 
 
@@ -92,10 +92,8 @@
     own_kv.start()
 
     backs = [0, 7 - 6 * side, 8]
-    slots = [0, 3 - 2 * side, 2]
-    for place_at, offset in enumerate(OFFSETS):
+    for offset in OFFSETS:
         backs += [2 * offset, 2 * offset - 1 + 2 * side]
-        slots += [4 + 2 * place_at, 5 + 2 * place_at]
 
     own_block = chip * 2 + core
     for i in range(CHUNKS):
@@ -178,57 +176,54 @@
     scale = 1.0 / math.sqrt(128)
     tiles = block * 8 // TILE
 
-    def run(stage, t):
-        first, last = stage == 0, stage == len(STAGES) - 1
-        used = STAGES[stage]
+    def run(t, used, places, first):
         ones = jnp.ones((16, len(used) * 2 * block), BF16)
-        units = [(r, h) for r in range(tiles) for h in (0, 1)]
-
-        def score(r, h):
-            at = slice(r * TILE, (r + 1) * TILE)
-            rhs = jnp.concatenate([qbuf[t, h, :, at], hot[:, at]], axis=0)
-            keys = jnp.concatenate(
-                [kvbuf[slots[i], which, 0, h] for i in used for which in (0, 1)], axis=0)
-            masks = jnp.concatenate([bias[t, i] for i in used], axis=0)
-            return jnp.dot(jnp.concatenate([keys, masks], axis=1), rhs, preferred_element_type=F32)
-
-        done = []
-        ready = score(*units[0])
-        for n, (r, h) in enumerate(units):
-            at = slice(r * TILE, (r + 1) * TILE)
-            scores = ready
-            if n + 1 < len(units):
-                ready = score(*units[n + 1])
-            new_top = jnp.max(scores, axis=0, keepdims=True)
-            if not first:
-                old_top = top[t, h, 0:1, at]
-                new_top = jnp.maximum(old_top, new_top)
-            weights = jnp.exp((scores - new_top) * scale).astype(BF16)
-            values = jnp.concatenate(
-                [kvbuf[slots[i], which, 1, h] for i in used for which in (0, 1)], axis=1)
-            total = jnp.dot(jnp.concatenate([values, ones], axis=0), weights,
-                            preferred_element_type=F32)
-            if not first:
-                total = total + acc[t, h, :, at] * jnp.exp((old_top - new_top) * scale)
-            if last:
-                result = total[:128] / total[128:129]
-                done.append(result.T.reshape(TILE // 8, 8, 128))
-                if h == 1:
-                    both = jnp.concatenate(done[-2:], axis=1).astype(BF16)
-                    ostage[t, r * (TILE // 8):(r + 1) * (TILE // 8)] = both
-            else:
+
+        def step(j, _):
+            units = [(pl.ds(pl.multiple_of((j * TOGETHER + r) * TILE, TILE), TILE), h)
+                     for r in range(TOGETHER) for h in (0, 1)]
+
+            def score(at, h):
+                rhs = jnp.concatenate([qbuf[t, h, :, at], hot[:, at]], axis=0)
+                keys = jnp.concatenate(
+                    [kvbuf[slot, which, 0, h] for slot in places for which in (0, 1)], axis=0)
+                masks = jnp.concatenate([bias[t, i] for i in used], axis=0)
+                return jnp.dot(jnp.concatenate([keys, masks], axis=1), rhs,
+                               preferred_element_type=F32)
+
+            ready = score(*units[0])
+            for n, (at, h) in enumerate(units):
+                scores = ready
+                if n + 1 < len(units):
+                    ready = score(*units[n + 1])
+                new_top = jnp.max(scores, axis=0, keepdims=True)
+                if not first:
+                    old_top = top[t, h, 0:1, at]
+                    new_top = jnp.maximum(old_top, new_top)
+                weights = jnp.exp((scores - new_top) * scale).astype(BF16)
+                values = jnp.concatenate(
+                    [kvbuf[slot, which, 1, h] for slot in places for which in (0, 1)], axis=1)
+                total = jnp.dot(jnp.concatenate([values, ones], axis=0), weights,
+                                preferred_element_type=F32)
+                if not first:
+                    total = total + acc[t, h, :, at] * jnp.exp((old_top - new_top) * scale)
                 acc[t, h, :, at] = total
                 top[t, h, 0:1, at] = new_top
-
-    def run_both(stage, between=None):
-        def step(t, _):
-            run(stage, t)
-            if between is not None:
-                @pl.when(t == 0)
-                def _():
-                    between()
             return 0
-        lax.fori_loop(0, 2, step, 0)
+
+        lax.fori_loop(0, tiles // TOGETHER, step, 0)
+
+    def finish(t):
+        def step(r, _):
+            at = pl.ds(pl.multiple_of(r * TILE, TILE), TILE)
+            done = []
+            for h in (0, 1):
+                result = acc[t, h, :128, at] / acc[t, h, 128:129, at]
+                done.append(result.T.reshape(TILE // 8, 8, 128))
+            to = pl.ds(pl.multiple_of(r * (TILE // 8), TILE // 8), TILE // 8)
+            ostage[t, to] = jnp.concatenate(done, axis=1).astype(BF16)
+            return 0
+        lax.fori_loop(0, tiles, step, 0)
 
     def start_own(early):
         for i in (2, 0, 1):
@@ -265,31 +260,51 @@
     for which in (0, 1):
         arrived(kvbuf.at[X_TRANSIT, which], one_recv.at[0, which])
     pass_x.start()
-    run_both(0, previous)
+    run(other, [0], [0], True)
+    previous()
+    run(core, [0], [0], True)
     arrived(kvbuf.at[1], pass_recv.at[0])
     before(3)
     for i in (2, 0, 1):
         along(i, 1).start()
-    run_both(1, lambda: hand_on(0))
-    hand_on(1)
-    for stage in (2, 3):
-        for cross in (0, 1):
-            arrived(kvbuf.at[2 * stage + cross], two_recv.at[stage - 2, cross])
-        run_both(stage)
-    for cross in (0, 1):
-        arrived(kvbuf.at[8 + cross], pass_recv.at[1 + cross])
-
-    def finish(t, _):
-        t = jnp.where(t == 0, other, core)
-        run(4, t)
-
-        @pl.when(t == other)
-        def _():
+
+    def half_stage(n, _):
+        stage = n // 2
+        t = jnp.where(lax.rem(n, 2) == 0, other, core)
+
+        @pl.when(n == 1)
+        def _():
+            hand_on(0)
+
+        @pl.when(n == 2)
+        def _():
+            hand_on(1)
+            for cross in (0, 1):
+                arrived(kvbuf.at[4 + cross], two_recv.at[0, cross])
+
+        @pl.when(n == 4)
+        def _():
+            for cross in (0, 1):
+                arrived(kvbuf.at[6 + cross], two_recv.at[1, cross])
+
+        @pl.when(n == 6)
+        def _():
+            for cross in (0, 1):
+                arrived(kvbuf.at[8 + cross], pass_recv.at[1 + cross])
+
+        @pl.when(n == 7)
+        def _():
+            finish(other)
             remote(ostage.at[other], out_hbm.at[:, half(core), :],
                    mate_send.at[3], mate_recv.at[3], mate).start()
+
+        left = jnp.where(stage == 0, 3 - 2 * side, 2 * stage + 2)
+        right = jnp.where(stage == 0, 2, 2 * stage + 3)
+        run(t, [2 * stage + 1, 2 * stage + 2], [left, right], False)
         return 0
 
-    lax.fori_loop(0, 2, finish, 0)
+    lax.fori_loop(0, 8, half_stage, 0)
+    finish(core)
     own_out = pltpu.make_async_copy(ostage.at[core], out_hbm.at[:, half(core), :], here.at[0])
     own_out.start()
     for send in sends:

time: 50.2 us -> 53.3 us (1.062)
  Pallas kernels: 46.4 us -> 49.6 us
    pallas_call x1, Pallas kernels: 46.4 us -> 49.6 us  [local(): pl.pallas_call(functools.partial(kernel, rows, cols), out_shape=jax.Shape...]
where the time goes in v4:
time: 53.3 us; the launch traced here: 53.2 us
  Pallas kernels  49.6 us (93%)
  local copies, waits for them, and re-layouts  3.54 us (7%)
    pallas_call x1, Pallas kernels, local(): pl.pallas_call(functools.partial(kernel, rows, cols), out_shape=jax.Shape...  49.6 us
    unnamed x9, local copies, waits for them, and re-layouts  3.54 us

profile of v4, /device:TPU:2, one launch (start us, length us, event | category | flops | bytes accessed | tf_op | source)
XLA Modules:
  0.0 53.2 jit_solution(13473532713659635186)
XLA Ops:
  0.0 0.0 copy-start
  0.0 1.0 %copy.6 = bf16[128,4,128]{2,0,1:T(8,128)(2,1)S(1)} copy(bf16[128,4,128]{2,1,0:T(4,128)(2,1)} %param.6) | data formatting | bytes 262144 | tf_op args[1]
  1.0 0.9 %copy.7 = bf16[128,4,128]{2,0,1:T(8,128)(2,1)S(1)} copy(bf16[128,4,128]{2,1,0:T(4,128)(2,1)} %param.7) | data formatting | bytes 262144 | tf_op args[2]
  1.9 0.0 copy-start.1
  2.0 0.0 copy-start.2
  2.0 0.0 copy-done
  2.0 0.6 %copy-done.1 = s32[1,512]{1,0:T(1,128)S(1)} copy-done((s32[1,512]{1,0:T(1,128)S(1)}, s32[1,512]{1,0:T(1,128)}, u32[]{:S(2)}) %copy-start.1) | copy-done | bytes 2072
  2.6 0.0 copy-done.2
  2.6 49.6 %shard_map.55 = bf16[128,32,128]{2,1,0:T(8,128)(2,1)S(1)} custom-call(bf16[128,32,128]{2,1,0:T(8,128)(2,1)S(1)} %copy-done, bf16[2,2,2,128,128]{4,3,2,1,0:T(8,128)(2,1)S(1)} %maximum_bitcast_fusion.kv_ref, s32[1,128]{1,0:T(1,128)S(1)} %bitcast.5, s32[1,512]{1,0:T(1,128)S(1)} %copy-done.1), custom_call_target="tpu_custom_call" | custom-call | flops 10000000000 | bytes 8000000 | tf_op jit(solution)/shard_map/pallas_call | solution.py:337
  52.2 1.0 %copy.9 = bf16[128,32,128]{2,1,0:T(8,128)(2,1)} copy(bf16[128,32,128]{2,1,0:T(8,128)(2,1)S(1)} %shard_map.55) | data formatting | bytes 2097152
  (1 shorter events, 0.0 us)
Async XLA Ops:
  0.0 2.0 %copy-start = (bf16[128,32,128]{2,1,0:T(8,128)(2,1)S(1)}, bf16[128,32,128]{2,1,0:T(8,128)(2,1)}, u32[]{:S(2)}) copy-start(bf16[128,32,128]{2,1,0:T(8,128)(2,1)} %q_hbm.1) | copy-start | bytes 3145732
  1.9 0.7 %copy-start.1 = (s32[1,512]{1,0:T(1,128)S(1)}, s32[1,512]{1,0:T(1,128)}, u32[]{:S(2)}) copy-start(s32[1,512]{1,0:T(1,128)} %keep_ref.1) | copy-start | bytes 6148
  2.0 0.7 %copy-start.2 = (s32[128]{0:T(128)S(1)}, s32[128]{0:T(128)}, u32[]{:S(2)}) copy-start(s32[128]{0:T(128)} %param.8) | copy-start | bytes 1540

commit v5 on v2

--- a/solution.py
+++ b/solution.py
@@ -13,12 +13,12 @@
 OFFSETS = (1, 3, 2)
 X_TRANSIT, Y_TRANSIT = 10, 11
 CHUNKS = 9
-TILE = 512
+TILE = 256
 F32, BF16 = jnp.float32, jnp.bfloat16
 
 
 def kernel(rows, cols, q_hbm, kv_ref, start_ref, keep_ref, out_hbm,
-           kvbuf, kvs, qraw, meta, qbuf, hot, bias, acc, top, ostage,
+           kvbuf, kvs, qraw, meta, qbuf, hot, bias, acc, top, sbuf, wbuf, ostage,
            one_send, one_recv, two_send, two_recv, pass_send, pass_recv,
            mate_send, mate_recv, here):
     block = q_hbm.shape[0]
@@ -175,41 +175,45 @@
             return 0
         lax.fori_loop(0, block // 64, piece, 0)
 
-    scale = 1.0 / math.sqrt(128)
+    scale = math.log2(math.e) / math.sqrt(128)
     tiles = block * 8 // TILE
 
     def run(stage, t):
         first, last = stage == 0, stage == len(STAGES) - 1
         used = STAGES[stage]
-        ones = jnp.ones((16, len(used) * 2 * block), BF16)
+        span = len(used) * 2 * block
+        ones = jnp.ones((16, span), BF16)
         units = [(r, h) for r in range(tiles) for h in (0, 1)]
 
-        def score(r, h):
+        def score(n):
+            r, h = units[n]
             at = slice(r * TILE, (r + 1) * TILE)
             rhs = jnp.concatenate([qbuf[t, h, :, at], hot[:, at]], axis=0)
             keys = jnp.concatenate(
                 [kvbuf[slots[i], which, 0, h] for i in used for which in (0, 1)], axis=0)
             masks = jnp.concatenate([bias[t, i] for i in used], axis=0)
-            return jnp.dot(jnp.concatenate([keys, masks], axis=1), rhs, preferred_element_type=F32)
+            scores = jnp.dot(jnp.concatenate([keys, masks], axis=1), rhs,
+                             preferred_element_type=F32)
+            sbuf[n % 2, :span] = scores
+            return jnp.max(scores, axis=0, keepdims=True)
 
         done = []
-        ready = score(*units[0])
+        ready = score(0)
         for n, (r, h) in enumerate(units):
             at = slice(r * TILE, (r + 1) * TILE)
-            scores = ready
+            new_top = ready
             if n + 1 < len(units):
-                ready = score(*units[n + 1])
-            new_top = jnp.max(scores, axis=0, keepdims=True)
+                ready = score(n + 1)
             if not first:
                 old_top = top[t, h, 0:1, at]
                 new_top = jnp.maximum(old_top, new_top)
-            weights = jnp.exp((scores - new_top) * scale).astype(BF16)
+            wbuf[n % 2, :span] = jnp.exp2((sbuf[n % 2, :span] - new_top) * scale).astype(BF16)
             values = jnp.concatenate(
                 [kvbuf[slots[i], which, 1, h] for i in used for which in (0, 1)], axis=1)
-            total = jnp.dot(jnp.concatenate([values, ones], axis=0), weights,
+            total = jnp.dot(jnp.concatenate([values, ones], axis=0), wbuf[n % 2, :span],
                             preferred_element_type=F32)
             if not first:
-                total = total + acc[t, h, :, at] * jnp.exp((old_top - new_top) * scale)
+                total = total + acc[t, h, :, at] * jnp.exp2((old_top - new_top) * scale)
             if last:
                 result = total[:128] / total[128:129]
                 done.append(result.T.reshape(TILE // 8, 8, 128))
@@ -334,6 +338,8 @@
             pltpu.VMEM((2, CHUNKS, 2 * block, block), BF16),
             pltpu.VMEM((2, 2, 144, block * 8), F32),
             pltpu.VMEM((2, 2, 8, block * 8), F32),
+            pltpu.VMEM((2, 4 * block, TILE), F32),
+            pltpu.VMEM((2, 4 * block, TILE), BF16),
             pltpu.VMEM((2, block, 16, 128), BF16),
             pltpu.SemaphoreType.DMA((3, 2)),
             pltpu.SemaphoreType.DMA((3, 2)),

time: 50.2 us -> 50.5 us (level)
  no operation moved by 1% of the time
where the time goes in v5:
time: 50.5 us; the launch traced here: 50.3 us
  Pallas kernels  46.7 us (92%)
  local copies, waits for them, and re-layouts  3.54 us (7%)
    pallas_call x1, Pallas kernels, local(): pl.pallas_call(functools.partial(kernel, rows, cols), out_shape=jax.Shape...  46.7 us
    unnamed x9, local copies, waits for them, and re-layouts  3.54 us

profile of v5, /device:TPU:2, one launch (start us, length us, event | category | flops | bytes accessed | tf_op | source)
XLA Modules:
  0.0 50.3 jit_solution(8068640443573739504)
XLA Ops:
  0.0 0.0 copy-start
  0.0 1.0 %copy.6 = bf16[128,4,128]{2,0,1:T(8,128)(2,1)S(1)} copy(bf16[128,4,128]{2,1,0:T(4,128)(2,1)} %param.6) | data formatting | bytes 262144 | tf_op args[1]
  1.0 0.9 %copy.7 = bf16[128,4,128]{2,0,1:T(8,128)(2,1)S(1)} copy(bf16[128,4,128]{2,1,0:T(4,128)(2,1)} %param.7) | data formatting | bytes 262144 | tf_op args[2]
  1.9 0.0 copy-start.1
  2.0 0.0 copy-start.2
  2.0 0.0 copy-done
  2.0 0.6 %copy-done.1 = s32[1,512]{1,0:T(1,128)S(1)} copy-done((s32[1,512]{1,0:T(1,128)S(1)}, s32[1,512]{1,0:T(1,128)}, u32[]{:S(2)}) %copy-start.1) | copy-done | bytes 2072
  2.6 0.0 copy-done.2
  2.6 46.7 %shard_map.55 = bf16[128,32,128]{2,1,0:T(8,128)(2,1)S(1)} custom-call(bf16[128,32,128]{2,1,0:T(8,128)(2,1)S(1)} %copy-done, bf16[2,2,2,128,128]{4,3,2,1,0:T(8,128)(2,1)S(1)} %maximum_bitcast_fusion.kv_ref, s32[1,128]{1,0:T(1,128)S(1)} %bitcast.5, s32[1,512]{1,0:T(1,128)S(1)} %copy-done.1), custom_call_target="tpu_custom_call" | custom-call | flops 10000000000 | bytes 8000000 | tf_op jit(solution)/shard_map/pallas_call | solution.py:326
  49.3 1.0 %copy.9 = bf16[128,32,128]{2,1,0:T(8,128)(2,1)} copy(bf16[128,32,128]{2,1,0:T(8,128)(2,1)S(1)} %shard_map.55) | data formatting | bytes 2097152
  (1 shorter events, 0.0 us)
Async XLA Ops:
  0.0 2.0 %copy-start = (bf16[128,32,128]{2,1,0:T(8,128)(2,1)S(1)}, bf16[128,32,128]{2,1,0:T(8,128)(2,1)}, u32[]{:S(2)}) copy-start(bf16[128,32,128]{2,1,0:T(8,128)(2,1)} %q_hbm.1) | copy-start | bytes 3145732
  1.9 0.7 %copy-start.1 = (s32[1,512]{1,0:T(1,128)S(1)}, s32[1,512]{1,0:T(1,128)}, u32[]{:S(2)}) copy-start(s32[1,512]{1,0:T(1,128)} %keep_ref.1) | copy-start | bytes 6148
  2.0 0.7 %copy-start.2 = (s32[128]{0:T(128)S(1)}, s32[128]{0:T(128)}, u32[]{:S(2)}) copy-start(s32[128]{0:T(128)} %param.8) | copy-start | bytes 1540

commit v6 on v5

--- a/solution.py
+++ b/solution.py
@@ -9,9 +9,9 @@
 from jax.sharding import PartitionSpec as P
 
 MASKED = -1e30
-STAGES = ((0,), (1, 2), (3, 4), (5, 6), (7, 8))
+STAGES = ((0,), (1, 2), (3, 5), (7, 4), (6, 8))
 OFFSETS = (1, 3, 2)
-X_TRANSIT, Y_TRANSIT = 10, 11
+X_TRANSIT, Y_TRANSIT, LATE_TRANSIT = 10, 11, 12
 CHUNKS = 9
 TILE = 256
 F32, BF16 = jnp.float32, jnp.bfloat16
@@ -144,9 +144,11 @@
 
     pass_x = remote(kvbuf.at[X_TRANSIT], kvbuf.at[1], pass_send.at[0], pass_recv.at[0],
                     beside(way, core))
-    pass_y = [remote(kvbuf.at[Y_TRANSIT + cross], kvbuf.at[8 + cross],
-                     pass_send.at[1 + cross], pass_recv.at[1 + cross], above(way))
-              for cross in (0, 1)]
+    pass_y = remote(kvbuf.at[Y_TRANSIT], kvbuf.at[8], pass_send.at[1], pass_recv.at[1], above(way))
+    late = remote(kvbuf.at[8], kvbuf.at[LATE_TRANSIT], two_send.at[2, 1], two_recv.at[2, 1],
+                  beside(way, core))
+    pass_late = remote(kvbuf.at[LATE_TRANSIT], kvbuf.at[9], pass_send.at[2], pass_recv.at[2],
+                       beside(way, core))
 
     group = lax.broadcasted_iota(jnp.int32, hot.shape, 1) // 8
     token = lax.broadcasted_iota(jnp.int32, hot.shape, 0)
@@ -242,9 +244,17 @@
             def _():
                 along(i, 0).start()
 
-    def hand_on(cross):
-        arrived(kvbuf.at[Y_TRANSIT + cross], two_recv.at[2, cross])
-        pass_y[cross].start()
+    def far():
+        arrived(kvbuf.at[Y_TRANSIT], two_recv.at[2, 0])
+        pass_y.start()
+
+    def far_here():
+        arrived(kvbuf.at[8], pass_recv.at[1])
+        late.start()
+
+    def far_on():
+        arrived(kvbuf.at[LATE_TRANSIT], two_recv.at[2, 1])
+        pass_late.start()
 
     def before(slot):
         @pl.when(col > 0)
@@ -272,16 +282,16 @@
     run_both(0, previous)
     arrived(kvbuf.at[1], pass_recv.at[0])
     before(3)
-    for i in (2, 0, 1):
+    for i in (0, 1):
         along(i, 1).start()
-    run_both(1, lambda: hand_on(0))
-    hand_on(1)
-    for stage in (2, 3):
-        for cross in (0, 1):
-            arrived(kvbuf.at[2 * stage + cross], two_recv.at[stage - 2, cross])
-        run_both(stage)
-    for cross in (0, 1):
-        arrived(kvbuf.at[8 + cross], pass_recv.at[1 + cross])
+    run_both(1, far)
+    for i in (0, 1):
+        arrived(kvbuf.at[4 + 2 * i], two_recv.at[i, 0])
+    run_both(2, far_here)
+    arrived(kvbuf.at[5], two_recv.at[0, 1])
+    run_both(3, far_on)
+    arrived(kvbuf.at[7], two_recv.at[1, 1])
+    arrived(kvbuf.at[9], pass_recv.at[2])
 
     def finish(t, _):
         t = jnp.where(t == 0, other, core)
@@ -305,10 +315,10 @@
             send.wait_send()
 
     for i in range(3):
-        for cross in (0, 1):
-            along(i, cross).wait_send()
-    pass_x.wait_send()
-    for copy in pass_y:
+        along(i, 0).wait_send()
+        if i < 2:
+            along(i, 1).wait_send()
+    for copy in (pass_x, pass_y, late, pass_late):
         copy.wait_send()
     own_out.wait()
     remote(ostage.at[other], out_hbm.at[:, half(core), :],

time: 50.5 us -> 53.1 us (1.051)
  the two profiles are of different devices: /device:TPU:2 before, /device:TPU:96 now
where the time goes in v6:
time: 53.1 us; the launch traced here: 53 us
  Pallas kernels  49.4 us (93%)
  local copies, waits for them, and re-layouts  3.54 us (7%)
    pallas_call x1, Pallas kernels, local(): pl.pallas_call(functools.partial(kernel, rows, cols), out_shape=jax.Shape...  49.4 us
    unnamed x9, local copies, waits for them, and re-layouts  3.54 us

profile of v6, /device:TPU:96, one launch (start us, length us, event | category | flops | bytes accessed | tf_op | source)
XLA Modules:
  0.0 53.0 jit_solution(6764074718098076378)
XLA Ops:
  0.0 0.0 copy-start
  0.0 1.0 %copy.6 = bf16[128,4,128]{2,0,1:T(8,128)(2,1)S(1)} copy(bf16[128,4,128]{2,1,0:T(4,128)(2,1)} %param.6) | data formatting | bytes 262144 | tf_op args[1]
  1.0 0.9 %copy.7 = bf16[128,4,128]{2,0,1:T(8,128)(2,1)S(1)} copy(bf16[128,4,128]{2,1,0:T(4,128)(2,1)} %param.7) | data formatting | bytes 262144 | tf_op args[2]
  1.9 0.0 copy-start.1
  2.0 0.0 copy-start.2
  2.0 0.0 copy-done
  2.0 0.6 %copy-done.1 = s32[1,512]{1,0:T(1,128)S(1)} copy-done((s32[1,512]{1,0:T(1,128)S(1)}, s32[1,512]{1,0:T(1,128)}, u32[]{:S(2)}) %copy-start.1) | copy-done | bytes 2072
  2.6 0.0 copy-done.2
  2.6 49.4 %shard_map.55 = bf16[128,32,128]{2,1,0:T(8,128)(2,1)S(1)} custom-call(bf16[128,32,128]{2,1,0:T(8,128)(2,1)S(1)} %copy-done, bf16[2,2,2,128,128]{4,3,2,1,0:T(8,128)(2,1)S(1)} %maximum_bitcast_fusion.kv_ref, s32[1,128]{1,0:T(1,128)S(1)} %bitcast.5, s32[1,512]{1,0:T(1,128)S(1)} %copy-done.1), custom_call_target="tpu_custom_call" | custom-call | flops 10000000000 | bytes 8000000 | tf_op jit(solution)/shard_map/pallas_call | solution.py:336
  52.0 1.0 %copy.9 = bf16[128,32,128]{2,1,0:T(8,128)(2,1)} copy(bf16[128,32,128]{2,1,0:T(8,128)(2,1)S(1)} %shard_map.55) | data formatting | bytes 2097152
  (1 shorter events, 0.0 us)
Async XLA Ops:
  0.0 2.0 %copy-start = (bf16[128,32,128]{2,1,0:T(8,128)(2,1)S(1)}, bf16[128,32,128]{2,1,0:T(8,128)(2,1)}, u32[]{:S(2)}) copy-start(bf16[128,32,128]{2,1,0:T(8,128)(2,1)} %q_hbm.1) | copy-start | bytes 3145732
  1.9 0.7 %copy-start.1 = (s32[1,512]{1,0:T(1,128)S(1)}, s32[1,512]{1,0:T(1,128)}, u32[]{:S(2)}) copy-start(s32[1,512]{1,0:T(1,128)} %keep_ref.1) | copy-start | bytes 6148
  2.0 0.7 %copy-start.2 = (s32[128]{0:T(128)S(1)}, s32[128]{0:T(128)}, u32[]{:S(2)}) copy-start(s32[128]{0:T(128)} %param.8) | copy-start | bytes 1540

commit v7 on v5

--- a/solution.py
+++ b/solution.py
@@ -9,7 +9,7 @@
 from jax.sharding import PartitionSpec as P
 
 MASKED = -1e30
-STAGES = ((0,), (1, 2), (3, 4), (5, 6), (7, 8))
+STAGES = ((0,), (2,), (1, 3), (5, 4), (6, 7), (8,))
 OFFSETS = (1, 3, 2)
 X_TRANSIT, Y_TRANSIT = 10, 11
 CHUNKS = 9
@@ -266,26 +266,32 @@
     arrived(qraw.at[other], mate_recv.at[1])
     make_bias(other)
     regroup(other)
-    for which in (0, 1):
-        arrived(kvbuf.at[X_TRANSIT, which], one_recv.at[0, which])
-    pass_x.start()
-    run_both(0, previous)
+    def across():
+        for which in (0, 1):
+            arrived(kvbuf.at[X_TRANSIT, which], one_recv.at[0, which])
+        pass_x.start()
+
+    run_both(0, across)
+    previous()
+    run_both(1)
     arrived(kvbuf.at[1], pass_recv.at[0])
     before(3)
     for i in (2, 0, 1):
         along(i, 1).start()
-    run_both(1, lambda: hand_on(0))
+    arrived(kvbuf.at[4], two_recv.at[0, 0])
+    run_both(2, lambda: hand_on(0))
     hand_on(1)
-    for stage in (2, 3):
-        for cross in (0, 1):
-            arrived(kvbuf.at[2 * stage + cross], two_recv.at[stage - 2, cross])
-        run_both(stage)
-    for cross in (0, 1):
-        arrived(kvbuf.at[8 + cross], pass_recv.at[1 + cross])
+    arrived(kvbuf.at[6], two_recv.at[1, 0])
+    arrived(kvbuf.at[5], two_recv.at[0, 1])
+    run_both(3)
+    arrived(kvbuf.at[7], two_recv.at[1, 1])
+    arrived(kvbuf.at[8], pass_recv.at[1])
+    run_both(4)
+    arrived(kvbuf.at[9], pass_recv.at[2])
 
     def finish(t, _):
         t = jnp.where(t == 0, other, core)
-        run(4, t)
+        run(5, t)
 
         @pl.when(t == other)
         def _():

time: 50.5 us -> 49.6 us (0.982); the launches traced: 50.3 us -> 48.9 us
  Pallas kernels: 46.7 us -> 45.3 us
    pallas_call x1, Pallas kernels: 46.7 us -> 45.3 us  [local(): pl.pallas_call(functools.partial(kernel, rows, cols), out_shape=jax.Shape...]
where the time goes in v7:
time: 49.6 us; the launch traced here: 48.9 us
  Pallas kernels  45.3 us (91%)
  local copies, waits for them, and re-layouts  3.54 us (7%)
    pallas_call x1, Pallas kernels, local(): pl.pallas_call(functools.partial(kernel, rows, cols), out_shape=jax.Shape...  45.3 us
    unnamed x9, local copies, waits for them, and re-layouts  3.54 us

profile of v7, /device:TPU:2, one launch (start us, length us, event | category | flops | bytes accessed | tf_op | source)
XLA Modules:
  0.0 48.9 jit_solution(3501560221415873929)
XLA Ops:
  0.0 0.0 copy-start
  0.0 1.0 %copy.6 = bf16[128,4,128]{2,0,1:T(8,128)(2,1)S(1)} copy(bf16[128,4,128]{2,1,0:T(4,128)(2,1)} %param.6) | data formatting | bytes 262144 | tf_op args[1]
  1.0 0.9 %copy.7 = bf16[128,4,128]{2,0,1:T(8,128)(2,1)S(1)} copy(bf16[128,4,128]{2,1,0:T(4,128)(2,1)} %param.7) | data formatting | bytes 262144 | tf_op args[2]
  1.9 0.0 copy-start.1
  2.0 0.0 copy-start.2
  2.0 0.0 copy-done
  2.0 0.6 %copy-done.1 = s32[1,512]{1,0:T(1,128)S(1)} copy-done((s32[1,512]{1,0:T(1,128)S(1)}, s32[1,512]{1,0:T(1,128)}, u32[]{:S(2)}) %copy-start.1) | copy-done | bytes 2072
  2.6 0.0 copy-done.2
  2.6 45.3 %shard_map.55 = bf16[128,32,128]{2,1,0:T(8,128)(2,1)S(1)} custom-call(bf16[128,32,128]{2,1,0:T(8,128)(2,1)S(1)} %copy-done, bf16[2,2,2,128,128]{4,3,2,1,0:T(8,128)(2,1)S(1)} %maximum_bitcast_fusion.kv_ref, s32[1,128]{1,0:T(1,128)S(1)} %bitcast.5, s32[1,512]{1,0:T(1,128)S(1)} %copy-done.1), custom_call_target="tpu_custom_call" | custom-call | flops 10000000000 | bytes 8000000 | tf_op jit(solution)/shard_map/pallas_call | solution.py:332
  47.9 1.0 %copy.9 = bf16[128,32,128]{2,1,0:T(8,128)(2,1)} copy(bf16[128,32,128]{2,1,0:T(8,128)(2,1)S(1)} %shard_map.55) | data formatting | bytes 2097152
  (1 shorter events, 0.0 us)
Async XLA Ops:
  0.0 2.0 %copy-start = (bf16[128,32,128]{2,1,0:T(8,128)(2,1)S(1)}, bf16[128,32,128]{2,1,0:T(8,128)(2,1)}, u32[]{:S(2)}) copy-start(bf16[128,32,128]{2,1,0:T(8,128)(2,1)} %q_hbm.1) | copy-start | bytes 3145732
  1.9 0.7 %copy-start.1 = (s32[1,512]{1,0:T(1,128)S(1)}, s32[1,512]{1,0:T(1,128)}, u32[]{:S(2)}) copy-start(s32[1,512]{1,0:T(1,128)} %keep_ref.1) | copy-start | bytes 6148
  2.0 0.7 %copy-start.2 = (s32[128]{0:T(128)S(1)}, s32[128]{0:T(128)}, u32[]{:S(2)}) copy-start(s32[128]{0:T(128)} %param.8) | copy-start | bytes 1540

commit v8 on v7

--- a/solution.py
+++ b/solution.py
@@ -207,7 +207,7 @@
             if not first:
                 old_top = top[t, h, 0:1, at]
                 new_top = jnp.maximum(old_top, new_top)
-            wbuf[n % 2, :span] = jnp.exp2((sbuf[n % 2, :span] - new_top) * scale).astype(BF16)
+            wbuf[n % 2, :span] = jnp.exp2(((sbuf[n % 2, :span] - new_top) * scale).astype(BF16))
             values = jnp.concatenate(
                 [kvbuf[slots[i], which, 1, h] for i in used for which in (0, 1)], axis=1)
             total = jnp.dot(jnp.concatenate([values, ones], axis=0), wbuf[n % 2, :span],

time: 49.6 us -> 50.4 us (1.016)
  Pallas kernels: 45.3 us -> 46 us
    pallas_call x1, Pallas kernels: 45.3 us -> 46 us  [local(): pl.pallas_call(functools.partial(kernel, rows, cols), out_shape=jax.Shape...]
where the time goes in v8:
time: 50.4 us; the launch traced here: 49.7 us
  Pallas kernels  46 us (91%)
  local copies, waits for them, and re-layouts  3.54 us (7%)
    pallas_call x1, Pallas kernels, local(): pl.pallas_call(functools.partial(kernel, rows, cols), out_shape=jax.Shape...  46 us
    unnamed x9, local copies, waits for them, and re-layouts  3.54 us

profile of v8, /device:TPU:2, one launch (start us, length us, event | category | flops | bytes accessed | tf_op | source)
XLA Modules:
  0.0 49.7 jit_solution(9957298598628497316)
XLA Ops:
  0.0 0.0 copy-start
  0.0 1.0 %copy.6 = bf16[128,4,128]{2,0,1:T(8,128)(2,1)S(1)} copy(bf16[128,4,128]{2,1,0:T(4,128)(2,1)} %param.6) | data formatting | bytes 262144 | tf_op args[1]
  1.0 0.9 %copy.7 = bf16[128,4,128]{2,0,1:T(8,128)(2,1)S(1)} copy(bf16[128,4,128]{2,1,0:T(4,128)(2,1)} %param.7) | data formatting | bytes 262144 | tf_op args[2]
  1.9 0.0 copy-start.1
  2.0 0.0 copy-start.2
  2.0 0.0 copy-done
  2.0 0.6 %copy-done.1 = s32[1,512]{1,0:T(1,128)S(1)} copy-done((s32[1,512]{1,0:T(1,128)S(1)}, s32[1,512]{1,0:T(1,128)}, u32[]{:S(2)}) %copy-start.1) | copy-done | bytes 2072
  2.6 0.0 copy-done.2
  2.6 46.0 %shard_map.55 = bf16[128,32,128]{2,1,0:T(8,128)(2,1)S(1)} custom-call(bf16[128,32,128]{2,1,0:T(8,128)(2,1)S(1)} %copy-done, bf16[2,2,2,128,128]{4,3,2,1,0:T(8,128)(2,1)S(1)} %maximum_bitcast_fusion.kv_ref, s32[1,128]{1,0:T(1,128)S(1)} %bitcast.5, s32[1,512]{1,0:T(1,128)S(1)} %copy-done.1), custom_call_target="tpu_custom_call" | custom-call | flops 10000000000 | bytes 8000000 | tf_op jit(solution)/shard_map/pallas_call | solution.py:332
  48.7 1.0 %copy.9 = bf16[128,32,128]{2,1,0:T(8,128)(2,1)} copy(bf16[128,32,128]{2,1,0:T(8,128)(2,1)S(1)} %shard_map.55) | data formatting | bytes 2097152
  (1 shorter events, 0.0 us)
Async XLA Ops:
  0.0 2.0 %copy-start = (bf16[128,32,128]{2,1,0:T(8,128)(2,1)S(1)}, bf16[128,32,128]{2,1,0:T(8,128)(2,1)}, u32[]{:S(2)}) copy-start(bf16[128,32,128]{2,1,0:T(8,128)(2,1)} %q_hbm.1) | copy-start | bytes 3145732
  1.9 0.7 %copy-start.1 = (s32[1,512]{1,0:T(1,128)S(1)}, s32[1,512]{1,0:T(1,128)}, u32[]{:S(2)}) copy-start(s32[1,512]{1,0:T(1,128)} %keep_ref.1) | copy-start | bytes 6148
  2.0 0.7 %copy-start.2 = (s32[128]{0:T(128)S(1)}, s32[128]{0:T(128)}, u32[]{:S(2)}) copy-start(s32[128]{0:T(128)} %param.8) | copy-start | bytes 1540

commit v9 on v7

--- a/solution.py
+++ b/solution.py
@@ -9,7 +9,7 @@
 from jax.sharding import PartitionSpec as P
 
 MASKED = -1e30
-STAGES = ((0,), (2,), (1, 3), (5, 4), (6, 7), (8,))
+STAGES = ((0,), (2,), (1,), (3, 5), (7, 4), (6, 8))
 OFFSETS = (1, 3, 2)
 X_TRANSIT, Y_TRANSIT = 10, 11
 CHUNKS = 9
@@ -178,10 +178,10 @@
     scale = math.log2(math.e) / math.sqrt(128)
     tiles = block * 8 // TILE
 
-    def run(stage, t):
+    def run(stage, t, parts=(0, 1)):
         first, last = stage == 0, stage == len(STAGES) - 1
         used = STAGES[stage]
-        span = len(used) * 2 * block
+        span = len(used) * len(parts) * block
         ones = jnp.ones((16, span), BF16)
         units = [(r, h) for r in range(tiles) for h in (0, 1)]
 
@@ -190,8 +190,10 @@
             at = slice(r * TILE, (r + 1) * TILE)
             rhs = jnp.concatenate([qbuf[t, h, :, at], hot[:, at]], axis=0)
             keys = jnp.concatenate(
-                [kvbuf[slots[i], which, 0, h] for i in used for which in (0, 1)], axis=0)
-            masks = jnp.concatenate([bias[t, i] for i in used], axis=0)
+                [kvbuf[slots[i], which, 0, h] for i in used for which in parts], axis=0)
+            masks = jnp.concatenate(
+                [bias[t, i, which * block:(which + 1) * block] for i in used for which in parts],
+                axis=0)
             scores = jnp.dot(jnp.concatenate([keys, masks], axis=1), rhs,
                              preferred_element_type=F32)
             sbuf[n % 2, :span] = scores
@@ -209,7 +211,7 @@
                 new_top = jnp.maximum(old_top, new_top)
             wbuf[n % 2, :span] = jnp.exp2((sbuf[n % 2, :span] - new_top) * scale).astype(BF16)
             values = jnp.concatenate(
-                [kvbuf[slots[i], which, 1, h] for i in used for which in (0, 1)], axis=1)
+                [kvbuf[slots[i], which, 1, h] for i in used for which in parts], axis=1)
             total = jnp.dot(jnp.concatenate([values, ones], axis=0), wbuf[n % 2, :span],
                             preferred_element_type=F32)
             if not first:
@@ -271,22 +273,25 @@
             arrived(kvbuf.at[X_TRANSIT, which], one_recv.at[0, which])
         pass_x.start()
 
-    run_both(0, across)
+    run(0, 0, (0,))
+    across()
+    run(0, 1)
     previous()
-    run_both(1)
+    run(1, 0)
+    run(1, 1, (1,))
     arrived(kvbuf.at[1], pass_recv.at[0])
     before(3)
     for i in (2, 0, 1):
         along(i, 1).start()
-    arrived(kvbuf.at[4], two_recv.at[0, 0])
-    run_both(2, lambda: hand_on(0))
-    hand_on(1)
-    arrived(kvbuf.at[6], two_recv.at[1, 0])
+    run_both(2)
+    hand_on(0)
+    for i in (0, 1):
+        arrived(kvbuf.at[4 + 2 * i], two_recv.at[i, 0])
+    run_both(3, lambda: hand_on(1))
+    arrived(kvbuf.at[8], pass_recv.at[1])
     arrived(kvbuf.at[5], two_recv.at[0, 1])
-    run_both(3)
+    run_both(4)
     arrived(kvbuf.at[7], two_recv.at[1, 1])
-    arrived(kvbuf.at[8], pass_recv.at[1])
-    run_both(4)
     arrived(kvbuf.at[9], pass_recv.at[2])
 
     def finish(t, _):

time: 49.6 us -> 49.3 us (level); the launches traced: 48.9 us -> 49.1 us
  no operation moved by 1% of the time
where the time goes in v9:
time: 49.3 us; the launch traced here: 49.1 us
  Pallas kernels  45.5 us (92%)
  local copies, waits for them, and re-layouts  3.54 us (7%)
    pallas_call x1, Pallas kernels, local(): pl.pallas_call(functools.partial(kernel, rows, cols), out_shape=jax.Shape...  45.5 us
    unnamed x9, local copies, waits for them, and re-layouts  3.54 us

profile of v9, /device:TPU:2, one launch (start us, length us, event | category | flops | bytes accessed | tf_op | source)
XLA Modules:
  0.0 49.1 jit_solution(12049591421947727318)
XLA Ops:
  0.0 0.0 copy-start
  0.0 1.0 %copy.6 = bf16[128,4,128]{2,0,1:T(8,128)(2,1)S(1)} copy(bf16[128,4,128]{2,1,0:T(4,128)(2,1)} %param.6) | data formatting | bytes 262144 | tf_op args[1]
  1.0 0.9 %copy.7 = bf16[128,4,128]{2,0,1:T(8,128)(2,1)S(1)} copy(bf16[128,4,128]{2,1,0:T(4,128)(2,1)} %param.7) | data formatting | bytes 262144 | tf_op args[2]
  1.9 0.0 copy-start.1
  2.0 0.0 copy-start.2
  2.0 0.0 copy-done
  2.0 0.6 %copy-done.1 = s32[1,512]{1,0:T(1,128)S(1)} copy-done((s32[1,512]{1,0:T(1,128)S(1)}, s32[1,512]{1,0:T(1,128)}, u32[]{:S(2)}) %copy-start.1) | copy-done | bytes 2072
  2.6 0.0 copy-done.2
  2.6 45.5 %shard_map.55 = bf16[128,32,128]{2,1,0:T(8,128)(2,1)S(1)} custom-call(bf16[128,32,128]{2,1,0:T(8,128)(2,1)S(1)} %copy-done, bf16[2,2,2,128,128]{4,3,2,1,0:T(8,128)(2,1)S(1)} %maximum_bitcast_fusion.kv_ref, s32[1,128]{1,0:T(1,128)S(1)} %bitcast.5, s32[1,512]{1,0:T(1,128)S(1)} %copy-done.1), custom_call_target="tpu_custom_call" | custom-call | flops 10000000000 | bytes 8000000 | tf_op jit(solution)/shard_map/pallas_call | solution.py:337
  48.2 1.0 %copy.9 = bf16[128,32,128]{2,1,0:T(8,128)(2,1)} copy(bf16[128,32,128]{2,1,0:T(8,128)(2,1)S(1)} %shard_map.55) | data formatting | bytes 2097152
  (1 shorter events, 0.0 us)
Async XLA Ops:
  0.0 2.0 %copy-start = (bf16[128,32,128]{2,1,0:T(8,128)(2,1)S(1)}, bf16[128,32,128]{2,1,0:T(8,128)(2,1)}, u32[]{:S(2)}) copy-start(bf16[128,32,128]{2,1,0:T(8,128)(2,1)} %q_hbm.1) | copy-start | bytes 3145732
  1.9 0.7 %copy-start.1 = (s32[1,512]{1,0:T(1,128)S(1)}, s32[1,512]{1,0:T(1,128)}, u32[]{:S(2)}) copy-start(s32[1,512]{1,0:T(1,128)} %keep_ref.1) | copy-start | bytes 6148
  2.0 0.7 %copy-start.2 = (s32[128]{0:T(128)S(1)}, s32[128]{0:T(128)}, u32[]{:S(2)}) copy-start(s32[128]{0:T(128)} %param.8) | copy-start | bytes 1540

commit v10 on v9

--- a/solution.py
+++ b/solution.py
@@ -125,12 +125,19 @@
             onward.append(remote(kvs.at[which], kvbuf.at[slot, core],
                                  one_send.at[slot - 1, which], one_recv.at[slot - 1, core],
                                  device(next_col, y, at_side, which)))
-    for send in sends:
-        send.start()
+    for number in (3, 4, 0, 1):
+        sends[number].start()
 
     @pl.when(col < cols - 1)
     def _():
-        for send in onward:
+        for send in onward[:2]:
+            send.start()
+
+    sends[2].start()
+
+    @pl.when(col < cols - 1)
+    def _():
+        for send in onward[2:]:
             send.start()
 
     def along(i, cross):

time: 49.3 us -> 49.3 us (level)
  no operation moved by 1% of the time
where the time goes in v10:
time: 49.3 us; the launch traced here: 49.1 us
  Pallas kernels  45.5 us (92%)
  local copies, waits for them, and re-layouts  3.54 us (7%)
    pallas_call x1, Pallas kernels, local(): pl.pallas_call(functools.partial(kernel, rows, cols), out_shape=jax.Shape...  45.5 us
    unnamed x9, local copies, waits for them, and re-layouts  3.54 us

profile of v10, /device:TPU:2, one launch (start us, length us, event | category | flops | bytes accessed | tf_op | source)
XLA Modules:
  0.0 49.1 jit_solution(3227771506588463274)
XLA Ops:
  0.0 0.0 copy-start
  0.0 1.0 %copy.6 = bf16[128,4,128]{2,0,1:T(8,128)(2,1)S(1)} copy(bf16[128,4,128]{2,1,0:T(4,128)(2,1)} %param.6) | data formatting | bytes 262144 | tf_op args[1]
  1.0 0.9 %copy.7 = bf16[128,4,128]{2,0,1:T(8,128)(2,1)S(1)} copy(bf16[128,4,128]{2,1,0:T(4,128)(2,1)} %param.7) | data formatting | bytes 262144 | tf_op args[2]
  1.9 0.0 copy-start.1
  2.0 0.0 copy-start.2
  2.0 0.0 copy-done
  2.0 0.6 %copy-done.1 = s32[1,512]{1,0:T(1,128)S(1)} copy-done((s32[1,512]{1,0:T(1,128)S(1)}, s32[1,512]{1,0:T(1,128)}, u32[]{:S(2)}) %copy-start.1) | copy-done | bytes 2072
  2.6 0.0 copy-done.2
  2.6 45.5 %shard_map.55 = bf16[128,32,128]{2,1,0:T(8,128)(2,1)S(1)} custom-call(bf16[128,32,128]{2,1,0:T(8,128)(2,1)S(1)} %copy-done, bf16[2,2,2,128,128]{4,3,2,1,0:T(8,128)(2,1)S(1)} %maximum_bitcast_fusion.kv_ref, s32[1,128]{1,0:T(1,128)S(1)} %bitcast.5, s32[1,512]{1,0:T(1,128)S(1)} %copy-done.1), custom_call_target="tpu_custom_call" | custom-call | flops 10000000000 | bytes 8000000 | tf_op jit(solution)/shard_map/pallas_call | solution.py:344
  48.1 1.0 %copy.9 = bf16[128,32,128]{2,1,0:T(8,128)(2,1)} copy(bf16[128,32,128]{2,1,0:T(8,128)(2,1)S(1)} %shard_map.55) | data formatting | bytes 2097152
  (1 shorter events, 0.0 us)
Async XLA Ops:
  0.0 2.0 %copy-start = (bf16[128,32,128]{2,1,0:T(8,128)(2,1)S(1)}, bf16[128,32,128]{2,1,0:T(8,128)(2,1)}, u32[]{:S(2)}) copy-start(bf16[128,32,128]{2,1,0:T(8,128)(2,1)} %q_hbm.1) | copy-start | bytes 3145732
  1.9 0.7 %copy-start.1 = (s32[1,512]{1,0:T(1,128)S(1)}, s32[1,512]{1,0:T(1,128)}, u32[]{:S(2)}) copy-start(s32[1,512]{1,0:T(1,128)} %keep_ref.1) | copy-start | bytes 6148
  2.0 0.7 %copy-start.2 = (s32[128]{0:T(128)S(1)}, s32[128]{0:T(128)}, u32[]{:S(2)}) copy-start(s32[128]{0:T(128)} %param.8) | copy-start | bytes 1540
